TPU v7x, 256 devices: a whole 4x4x8 slice. The times are simulated.
256 devices in a mesh: tm: 32 (over y_hi, z, core), region: 8 (over y_lo, x).
Axes of the slice: x: 4, y: 4 (y_hi: 2, y_lo: 2; y = y_hi * 2 + y_lo), z: 8, core: 2. Of those that a mesh axis runs over, the one named last changes fastest.
Arguments:
- flux_init: float32 [128, 256, 128], P('region', 'tm'), may hold values from -6 to 6
- penalty: float32 [128, 256, 128], P('region', 'tm'), may hold values from 0.05 to 0.5
- observed: float32 [262144], P(('tm', 'region')), may hold values from -12 to 12
- footprint: bfloat16 [10240, 128, 1024], P(('tm', 'region')), may hold values from -0.1875 to 0.1875
- tile_index: int32 [10240, 4], P(('tm', 'region')), may hold values from 0 to 127, as said below
Outputs:
- flux: float32 [128, 256, 128], P('region', 'tm')
Inputs may be any that keep to these rules, and one draw needn't show every extreme that they name: `tile_index`: each tile slot's entries are its observation block (below 8), how many windows back in time its flux block lies (below 4), its grid row (below 128) and a live flag of 0 or 1. On each device the live slots come first, at least half of its 40 slots are live, and some device has all 40 live.
All inputs are finite; a program needn't handle non-finite values.
Results may differ from a plain program's by a relative error of at most 0.0053.
Values may be sent and summed in bfloat16 or wider, within the bound.
A program may use at most 64 MiB of HBM per device.

v0:
```python
import math

import jax
import jax.numpy as jnp
from jax import lax
from jax.sharding import PartitionSpec as P

LAG = 4
ITERS = 2


def passed_along(block, axis, distance):
    devices = range(lax.axis_size(axis))
    route = [(i - distance, i) for i in devices if i - distance in devices]
    return lax.ppermute(block, axis, route)


def laid_out(pieces, dim):
    pieces = jnp.moveaxis(pieces, 0, dim)
    lengths = pieces.shape
    return pieces.reshape(*lengths[:dim], lengths[dim] * lengths[dim + 1], *lengths[dim + 2 :])


def sent_to_all(value, axis):
    length = lax.axis_size(axis)
    return lax.all_to_all(
        jnp.broadcast_to(value[None], (length, *value.shape)), axis, 0, 0, tiled=True
    )


def gather_directly(value, axis, dim):
    return laid_out(sent_to_all(value, axis), dim)


def sent_together(arrays, axis, dim, along):
    widths = [math.prod(a.shape[along:]) for a in arrays]
    both = jnp.concatenate(
        [a.reshape(*a.shape[:along], w) for a, w in zip(arrays, widths)], axis=along
    )
    filled = gather_directly(both, axis, dim)
    pieces = jnp.split(filled, [sum(widths[:k]) for k in range(1, len(widths))], axis=along)
    return tuple(
        (b.reshape(*filled.shape[:along], *a.shape[along:]) for a, b in zip(arrays, pieces))
    )


def padded_2(value, sides, width):
    edges = {}
    for axis, dim in sides:
        size, length = (lax.axis_size(axis), value.shape[dim])
        up = [(i, (i + 1) % size) for i in range(size - 1)]
        last = lax.slice_in_dim(value, length - width, length, axis=dim)
        first = lax.slice_in_dim(value, 0, width, axis=dim)
        edges[dim] = (
            lax.ppermute(last, axis, up),
            lax.ppermute(first, axis, [(b, a) for a, b in up]),
        )
    done = []
    for _, dim in sides:
        low, high = edges[dim]
        around = [(width, width) if d in done else (0, 0) for d in range(value.ndim)]
        value = jnp.concatenate([jnp.pad(low, around), value, jnp.pad(high, around)], axis=dim)
        done.append(dim)
    return value


def local(flux_init, penalty, observed, footprint, tile_index):
    regions = lax.axis_size("region")
    rows_here, hours_here, cells_across = flux_init.shape
    grid_rows = rows_here * regions
    tile_count, block_obs, panel_width = footprint.shape
    obs_blocks = observed.shape[0] // block_obs
    observed_blocks = observed.reshape(obs_blocks, block_obs)
    row_block = tile_index[:, 0]
    offset = tile_index[:, 1]
    grid_row = tile_index[:, 2]
    live_flag = tile_index[:, 3].astype(jnp.float32)
    selector = (row_block[:, None] == jnp.arange(obs_blocks, dtype=jnp.int32)[None, :]).astype(
        jnp.float32
    )
    picked = offset * grid_rows + grid_row
    first_row = lax.axis_index("region") * rows_here
    flux = flux_init
    for iteration in range(ITERS):
        flux_low = flux.astype(jnp.bfloat16)
        pieces = [flux_low] + [passed_along(flux_low, "tm", distance) for distance in range(1, LAG)]
        window = gather_directly(jnp.stack(pieces), "region", 1)
        block_table = window.reshape(LAG * grid_rows, panel_width)
        gathered_blocks = block_table[picked]
        products = (
            jnp.einsum("tok,tk->to", footprint, gathered_blocks, preferred_element_type=jnp.float32)
            * live_flag[:, None]
        )
        predicted = jnp.dot(selector.T, products, precision=lax.Precision.HIGHEST)
        residual = (predicted - observed_blocks).astype(jnp.bfloat16)
        spread = residual[row_block]
        tile_terms = (
            jnp.einsum("tok,to->tk", footprint, spread, preferred_element_type=jnp.float32)
            * live_flag[:, None]
        )
        all_terms, all_targets = sent_together(
            (tile_terms, picked.astype(jnp.float32)), "region", 0, 1
        )
        targets = all_targets.astype(jnp.int32)
        lag_of = targets // grid_rows
        local_row = targets % grid_rows - first_row
        inside = (local_row >= 0) & (local_row < rows_here)
        segment = jnp.where(inside, lag_of * rows_here + local_row, LAG * rows_here)
        summed = jax.ops.segment_sum(all_terms, segment, num_segments=LAG * rows_here + 1)
        reduced = summed[: LAG * rows_here].reshape(LAG, rows_here, hours_here, cells_across)
        adjoint = reduced[0]
        for distance in range(1, LAG):
            adjoint = adjoint + passed_along(reduced[distance], "tm", -distance)
        padded = padded_2(flux, (("tm", 1), ("region", 0)), 1)
        neighbours = padded[2:, 1:-1] + padded[:-2, 1:-1] + padded[1:-1, 2:] + padded[1:-1, :-2]
        along_cells = jnp.pad(flux, ((0, 0), (0, 0), (1, 1)))
        neighbours = neighbours + along_cells[:, :, 2:] + along_cells[:, :, :-2]
        laplace = 6.0 * flux - neighbours
        stepped = flux - 0.5 * (adjoint + 0.2 * laplace)
        cutoff = 0.5 * penalty
        flux = stepped - jnp.clip(stepped, -cutoff, cutoff)
    return flux


def solution(mesh):
    in_specs = (
        P("region", "tm", None),
        P("region", "tm", None),
        P(("tm", "region")),
        P(("tm", "region"), None, None),
        P(("tm", "region"), None),
    )
    out_specs = P("region", "tm", None)
    return jax.shard_map(local, mesh=mesh, in_specs=in_specs, out_specs=out_specs, check_vma=False)
```

profile of v0, /device:TPU:225, one launch (start us, length us, event | category | flops | bytes accessed | tf_op | source)
XLA Modules:
  0.0 192.4 jit_solution(4900753008183271710)
XLA Ops:
  0.0 0.8 convert_element_type.38
  0.8 2.2 %collective-permute-start = (bf16[16,8,128]{2,1,0:T(8,128)(2,1)S(1)}, bf16[16,8,128]{2,1,0:T(8,128)(2,1)S(1)}, u32[]{:S(2)}, u32[]{:S(2)}) collective-permute-start(bf16[16,8,128]{2,1,0:T(8,128)(2,1)S(1)} %convert_element_type.38), channel_id=1, source_target_pairs={{0,8},{8,16},{16,24},{24,32},{32,40},{40,48},{48,56},{56,64},{64,7... | collective-permute-start | bytes 98312 | tf_op jit(solution)/shard_map/ppermute | solution.py:15
  3.0 3.5 %collective-permute-start.1 = (bf16[16,8,128]{2,1,0:T(8,128)(2,1)S(1)}, bf16[16,8,128]{2,1,0:T(8,128)(2,1)S(1)}, u32[]{:S(2)}, u32[]{:S(2)}) collective-permute-start(bf16[16,8,128]{2,1,0:T(8,128)(2,1)S(1)} %convert_element_type.38), channel_id=1, source_target_pairs={{0,16},{8,24},{16,32},{24,40},{32,48},{40,56},{48,64},{56,72},{64,... | collective-permute-start | bytes 98312 | tf_op jit(solution)/shard_map/ppermute | solution.py:15
  6.6 3.6 %collective-permute-start.2 = (bf16[16,8,128]{2,1,0:T(8,128)(2,1)S(1)}, bf16[16,8,128]{2,1,0:T(8,128)(2,1)S(1)}, u32[]{:S(2)}, u32[]{:S(2)}) collective-permute-start(bf16[16,8,128]{2,1,0:T(8,128)(2,1)S(1)} %convert_element_type.38), channel_id=1, source_target_pairs={{0,24},{8,32},{16,40},{24,48},{32,56},{40,64},{48,72},{56,80},{64,... | collective-permute-start | bytes 98312 | tf_op jit(solution)/shard_map/ppermute | solution.py:15
  10.2 0.8 convert_bitcast_fusion.1
  11.0 0.8 collective-permute-done.2
  11.9 1.2 broadcast_in_dim.12
  13.1 4.6 %all-to-all-start = ((bf16[8,4,16,8,128]{4,3,2,1,0:T(8,128)(2,1)}), bf16[8,4,16,8,128]{4,3,2,1,0:T(8,128)(2,1)S(1)}, u32[]{:S(2)}, u32[]{:S(2)}) async-start(bf16[8,4,16,8,128]{4,3,2,1,0:T(8,128)(2,1)} %broadcast_in_dim.12), calls=%async_computation | async-start | bytes 2097152 | tf_op jit(solution)/shard_map/all_to_all | solution.py:26
  17.8 15.7 %all-to-all-done = bf16[8,4,16,8,128]{4,3,2,1,0:T(8,128)(2,1)S(1)} async-done(((bf16[8,4,16,8,128]{4,3,2,1,0:T(8,128)(2,1)}), bf16[8,4,16,8,128]{4,3,2,1,0:T(8,128)(2,1)S(1)}, u32[]{:S(2)}, u32[]{:S(2)}) %all-to-all-start) | async-done | bytes 1048608 | tf_op jit(solution)/shard_map/all_to_all | solution.py:26
  33.9 0.7 gather_fusion
  34.6 5.5 %fusion.18 = f32[40,1,128]{2,1,0:T(1,128)S(1)} fusion(bf16[40,128,1024]{2,1,0:T(8,128)(2,1)} %param.8, bf16[40,1024,1]{1,0,2:T(8,128)(2,1)S(1)} %bitcast.104), kind=kOutput, calls=%fused_computation.44 | convolution fusion | flops 10485760 | bytes 10588160 | tf_op jit(solution)/shard_map/tok,tk->to/dot_general | solution.py:91
  40.4 0.6 gather_fusion.1
  41.0 5.4 %fusion.56 = f32[40,1,1024]{2,1,0:T(1,128)S(1)} fusion(bf16[40,128,1024]{2,1,0:T(8,128)(2,1)} %param.8, bf16[40,128,1]{1,0,2:T(8,128)(2,1)S(1)} %bitcast.106), kind=kOutput, calls=%fused_computation.120 | convolution fusion | flops 10485760 | bytes 10659840 | tf_op jit(solution)/shard_map/tok,to->tk/dot_general | solution.py:98
  46.5 1.2 broadcast_in_dim.13
  47.8 3.7 %all-to-all-start.1 = ((f32[8,40,1025]{2,1,0:T(8,128)}), f32[8,40,1025]{2,1,0:T(8,128)S(1)}, u32[]{:S(2)}, u32[]{:S(2)}) async-start(f32[8,40,1025]{2,1,0:T(8,128)} %broadcast_in_dim.13), calls=%async_computation.1 | async-start | bytes 2949120 | tf_op jit(solution)/shard_map/all_to_all | solution.py:26
  51.5 1.3 collective-permute-start.8
  52.8 4.0 %collective-permute-start.9 = (f32[1,8,128]{2,1,0:T(8,128)S(1)}, f32[1,8,128]{2,1,0:T(8,128)S(1)}, u32[]{:S(2)}, u32[]{:S(2)}) collective-permute-start(f32[1,8,128]{2,1,0:T(8,128)S(1)} %get-tuple-element.22), channel_id=1, source_target_pairs={{0,1},{1,2},{2,3},{3,4},{4,5},{5,6},{6,7},{8,9},{9,10},{10,11},{11... | collective-permute-start | bytes 12296 | tf_op jit(solution)/shard_map/ppermute | solution.py:55
  56.9 15.0 %all-to-all-done.1 = f32[8,40,1025]{2,1,0:T(8,128)S(1)} async-done(((f32[8,40,1025]{2,1,0:T(8,128)}), f32[8,40,1025]{2,1,0:T(8,128)S(1)}, u32[]{:S(2)}, u32[]{:S(2)}) %all-to-all-start.1) | async-done | bytes 1312032 | tf_op jit(solution)/shard_map/all_to_all | solution.py:26
  72.1 3.3 %scatter_custom_fusion = f32[65,1024]{1,0:T(8,128)S(1)} fusion(s32[320]{0:T(512)S(1)} %fusion.10, f32[320,1025]{1,0:T(8,128)S(1)} %bitcast.94, f32[]{:T(128)} %constant.51.clone.1), kind=kCustom, calls=%fused_computation.8 | custom fusion | flops 327680 | bytes 1576964 | tf_op jit(solution)/shard_map/scatter-add | solution.py:109
  75.5 2.7 %collective-permute-start.3 = (f32[16,8,128]{2,1,0:T(8,128)S(1)}, f32[16,8,128]{2,1,0:T(8,128)S(1)}, u32[]{:S(2)}, u32[]{:S(2)}) collective-permute-start(f32[16,8,128]{2,1,0:T(8,128)S(1)} %bitcast.108), channel_id=1, source_target_pairs={{8,0},{16,8},{24,16},{32,24},{40,32},{48,40},{56,48},{64,56},{72,6... | collective-permute-start | bytes 196616 | tf_op jit(solution)/shard_map/ppermute | solution.py:15
  78.2 2.4 %collective-permute-start.4 = (f32[16,8,128]{2,1,0:T(8,128)S(1)}, f32[16,8,128]{2,1,0:T(8,128)S(1)}, u32[]{:S(2)}, u32[]{:S(2)}) collective-permute-start(f32[16,8,128]{2,1,0:T(8,128)S(1)} %bitcast.110), channel_id=1, source_target_pairs={{16,0},{24,8},{32,16},{40,24},{48,32},{56,40},{64,48},{72,56},{80,... | collective-permute-start | bytes 196616 | tf_op jit(solution)/shard_map/ppermute | solution.py:15
  80.7 5.3 %collective-permute-start.5 = (f32[16,8,128]{2,1,0:T(8,128)S(1)}, f32[16,8,128]{2,1,0:T(8,128)S(1)}, u32[]{:S(2)}, u32[]{:S(2)}) collective-permute-start(f32[16,8,128]{2,1,0:T(8,128)S(1)} %bitcast.112), channel_id=1, source_target_pairs={{24,0},{32,8},{40,16},{48,24},{56,32},{64,40},{72,48},{80,56},{88,... | collective-permute-start | bytes 196616 | tf_op jit(solution)/shard_map/ppermute | solution.py:15
  86.1 5.0 %collective-permute-start.6 = (f32[16,1,128]{2,1,0:T(1,128)S(1)}, f32[16,1,128]{2,1,0:T(1,128)S(1)}, u32[]{:S(2)}, u32[]{:S(2)}) collective-permute-start(f32[16,1,128]{2,1,0:T(1,128)S(1)} %get-tuple-element.24), channel_id=1, source_target_pairs={{0,8},{8,16},{16,24},{24,32},{32,40},{40,48},{48,56},{56,64},{64,7... | collective-permute-start | bytes 24584 | tf_op jit(solution)/shard_map/ppermute | solution.py:55
  91.1 1.9 collective-permute-start.7
  93.1 6.6 %collective-permute-done.7 = f32[16,1,128]{2,1,0:T(1,128)S(1)} collective-permute-done((f32[16,1,128]{2,1,0:T(1,128)S(1)}, f32[16,1,128]{2,1,0:T(1,128)S(1)}, u32[]{:S(2)}, u32[]{:S(2)}) %collective-permute-start.7) | collective-permute-done | bytes 8224 | tf_op jit(solution)/shard_map/ppermute | solution.py:56
  99.9 1.9 %collective-permute-start.10 = (bf16[16,8,128]{2,1,0:T(8,128)(2,1)S(1)}, bf16[16,8,128]{2,1,0:T(8,128)(2,1)S(1)}, u32[]{:S(2)}, u32[]{:S(2)}) collective-permute-start(bf16[16,8,128]{2,1,0:T(8,128)(2,1)S(1)} %get-tuple-element.5), channel_id=1, source_target_pairs={{0,8},{8,16},{16,24},{24,32},{32,40},{40,48},{48,56},{56,64},{64,7... | collective-permute-start | bytes 98312 | tf_op jit(solution)/shard_map/ppermute | solution.py:15
  101.8 1.9 collective-permute-start.11
  103.7 1.9 collective-permute-start.12
  105.7 0.8 collective-permute-done.11
  106.5 3.2 %collective-permute-done.12 = bf16[16,8,128]{2,1,0:T(8,128)(2,1)S(1)} collective-permute-done((bf16[16,8,128]{2,1,0:T(8,128)(2,1)S(1)}, bf16[16,8,128]{2,1,0:T(8,128)(2,1)S(1)}, u32[]{:S(2)}, u32[]{:S(2)}) %collective-permute-start.12) | collective-permute-done | bytes 32800 | tf_op jit(solution)/shard_map/ppermute | solution.py:15
  109.9 17.2 %all_to_all.20 = bf16[8,4,16,8,128]{4,3,2,1,0:T(8,128)(2,1)S(1)} all-to-all(bf16[8,4,16,8,128]{4,3,2,1,0:T(8,128)(2,1)S(1)} %broadcast_in_dim.16), channel_id=1, replica_groups=mesh['tm'=32,'region'=8] {'region'}, dimensions={0} | all-to-all | bytes 2097152 | tf_op jit(solution)/shard_map/all_to_all | solution.py:26
  127.5 0.7 gather_fusion.2
  128.1 5.5 %fusion.16 = f32[40,1,128]{2,1,0:T(1,128)S(1)} fusion(bf16[40,128,1024]{2,1,0:T(8,128)(2,1)} %param.8, bf16[40,1024,1]{1,0,2:T(8,128)(2,1)S(1)} %bitcast.103), kind=kOutput, calls=%fused_computation.42 | convolution fusion | flops 10485760 | bytes 10588160 | tf_op jit(solution)/shard_map/tok,tk->to/dot_general | solution.py:91
  133.9 0.6 gather_fusion.3
  134.5 5.4 %fusion.54 = f32[40,1,1024]{2,1,0:T(1,128)S(1)} fusion(bf16[40,128,1024]{2,1,0:T(8,128)(2,1)} %param.8, bf16[40,128,1]{1,0,2:T(8,128)(2,1)S(1)} %bitcast.105), kind=kOutput, calls=%fused_computation.118 | convolution fusion | flops 10485760 | bytes 10659840 | tf_op jit(solution)/shard_map/tok,to->tk/dot_general | solution.py:98
  140.1 1.2 broadcast_in_dim.17
  141.3 3.6 %all-to-all-start.3 = ((f32[8,40,1025]{2,1,0:T(8,128)}), f32[8,40,1025]{2,1,0:T(8,128)S(1)}, u32[]{:S(2)}, u32[]{:S(2)}) async-start(f32[8,40,1025]{2,1,0:T(8,128)} %broadcast_in_dim.17), calls=%async_computation.3 | async-start | bytes 2949120 | tf_op jit(solution)/shard_map/all_to_all | solution.py:26
  144.9 1.3 collective-permute-start.18
  146.2 4.2 %collective-permute-start.19 = (f32[1,8,128]{2,1,0:T(8,128)S(1)}, f32[1,8,128]{2,1,0:T(8,128)S(1)}, u32[]{:S(2)}, u32[]{:S(2)}) collective-permute-start(f32[1,8,128]{2,1,0:T(8,128)S(1)} %get-tuple-element.18), channel_id=1, source_target_pairs={{0,1},{1,2},{2,3},{3,4},{4,5},{5,6},{6,7},{8,9},{9,10},{10,11},{11... | collective-permute-start | bytes 12296 | tf_op jit(solution)/shard_map/ppermute | solution.py:55
  150.4 14.8 %all-to-all-done.3 = f32[8,40,1025]{2,1,0:T(8,128)S(1)} async-done(((f32[8,40,1025]{2,1,0:T(8,128)}), f32[8,40,1025]{2,1,0:T(8,128)S(1)}, u32[]{:S(2)}, u32[]{:S(2)}) %all-to-all-start.3) | async-done | bytes 1312032 | tf_op jit(solution)/shard_map/all_to_all | solution.py:26
  165.5 3.3 %scatter_custom_fusion.1 = f32[65,1024]{1,0:T(8,128)S(1)} fusion(s32[320]{0:T(512)S(1)} %fusion.15, f32[320,1025]{1,0:T(8,128)S(1)} %bitcast.96, f32[]{:T(128)} %constant.51.clone.1), kind=kCustom, calls=%fused_computation.6 | custom fusion | flops 327680 | bytes 1576964 | tf_op jit(solution)/shard_map/scatter-add | solution.py:109
  168.9 2.8 %collective-permute-start.13 = (f32[16,8,128]{2,1,0:T(8,128)S(1)}, f32[16,8,128]{2,1,0:T(8,128)S(1)}, u32[]{:S(2)}, u32[]{:S(2)}) collective-permute-start(f32[16,8,128]{2,1,0:T(8,128)S(1)} %bitcast.109), channel_id=1, source_target_pairs={{8,0},{16,8},{24,16},{32,24},{40,32},{48,40},{56,48},{64,56},{72,6... | collective-permute-start | bytes 196616 | tf_op jit(solution)/shard_map/ppermute | solution.py:15
  171.6 2.4 %collective-permute-start.14 = (f32[16,8,128]{2,1,0:T(8,128)S(1)}, f32[16,8,128]{2,1,0:T(8,128)S(1)}, u32[]{:S(2)}, u32[]{:S(2)}) collective-permute-start(f32[16,8,128]{2,1,0:T(8,128)S(1)} %bitcast.111), channel_id=1, source_target_pairs={{16,0},{24,8},{32,16},{40,24},{48,32},{56,40},{64,48},{72,56},{80,... | collective-permute-start | bytes 196616 | tf_op jit(solution)/shard_map/ppermute | solution.py:15
  174.1 3.2 %collective-permute-start.15 = (f32[16,8,128]{2,1,0:T(8,128)S(1)}, f32[16,8,128]{2,1,0:T(8,128)S(1)}, u32[]{:S(2)}, u32[]{:S(2)}) collective-permute-start(f32[16,8,128]{2,1,0:T(8,128)S(1)} %bitcast.113), channel_id=1, source_target_pairs={{24,0},{32,8},{40,16},{48,24},{56,32},{64,40},{72,48},{80,56},{88,... | collective-permute-start | bytes 196616 | tf_op jit(solution)/shard_map/ppermute | solution.py:15
  177.3 5.8 %collective-permute-start.16 = (f32[16,1,128]{2,1,0:T(1,128)S(1)}, f32[16,1,128]{2,1,0:T(1,128)S(1)}, u32[]{:S(2)}, u32[]{:S(2)}) collective-permute-start(f32[16,1,128]{2,1,0:T(1,128)S(1)} %get-tuple-element.20), channel_id=1, source_target_pairs={{0,8},{8,16},{16,24},{24,32},{32,40},{40,48},{48,56},{56,64},{64,7... | collective-permute-start | bytes 24584 | tf_op jit(solution)/shard_map/ppermute | solution.py:55
  183.0 1.9 collective-permute-start.17
  185.0 6.6 %collective-permute-done.17 = f32[16,1,128]{2,1,0:T(1,128)S(1)} collective-permute-done((f32[16,1,128]{2,1,0:T(1,128)S(1)}, f32[16,1,128]{2,1,0:T(1,128)S(1)}, u32[]{:S(2)}, u32[]{:S(2)}) %collective-permute-start.17) | collective-permute-done | bytes 8224 | tf_op jit(solution)/shard_map/ppermute | solution.py:56
  191.6 0.8 minimum_subtract_fusion
  (57 shorter events, 2.8 us)
Async XLA Ops:
  0.8 10.2 %collective-permute-start = (bf16[16,8,128]{2,1,0:T(8,128)(2,1)S(1)}, bf16[16,8,128]{2,1,0:T(8,128)(2,1)S(1)}, u32[]{:S(2)}, u32[]{:S(2)}) collective-permute-start(bf16[16,8,128]{2,1,0:T(8,128)(2,1)S(1)} %convert_element_type.38), channel_id=1, source_target_pairs={{0,8},{8,16},{16,24},{24,32},{32,40},{40,48},{48,56},{56,64},{64,7... | collective-permute-start | bytes 98312 | tf_op jit(solution)/shard_map/ppermute | solution.py:15
  3.0 8.0 %collective-permute-start.1 = (bf16[16,8,128]{2,1,0:T(8,128)(2,1)S(1)}, bf16[16,8,128]{2,1,0:T(8,128)(2,1)S(1)}, u32[]{:S(2)}, u32[]{:S(2)}) collective-permute-start(bf16[16,8,128]{2,1,0:T(8,128)(2,1)S(1)} %convert_element_type.38), channel_id=1, source_target_pairs={{0,16},{8,24},{16,32},{24,40},{32,48},{40,56},{48,64},{56,72},{64,... | collective-permute-start | bytes 98312 | tf_op jit(solution)/shard_map/ppermute | solution.py:15
  6.6 5.2 %collective-permute-start.2 = (bf16[16,8,128]{2,1,0:T(8,128)(2,1)S(1)}, bf16[16,8,128]{2,1,0:T(8,128)(2,1)S(1)}, u32[]{:S(2)}, u32[]{:S(2)}) collective-permute-start(bf16[16,8,128]{2,1,0:T(8,128)(2,1)S(1)} %convert_element_type.38), channel_id=1, source_target_pairs={{0,24},{8,32},{16,40},{24,48},{32,56},{40,64},{48,72},{56,80},{64,... | collective-permute-start | bytes 98312 | tf_op jit(solution)/shard_map/ppermute | solution.py:15
  11.9 5.8 %copy-start.2 = (s32[40,4]{0,1:T(4,128)S(1)}, s32[40,4]{0,1:T(4,128)}, u32[]{:S(2)}) copy-start(s32[40,4]{0,1:T(4,128)} %param.9) | copy-start | bytes 1924
  13.1 20.4 %all-to-all-start = ((bf16[8,4,16,8,128]{4,3,2,1,0:T(8,128)(2,1)}), bf16[8,4,16,8,128]{4,3,2,1,0:T(8,128)(2,1)S(1)}, u32[]{:S(2)}, u32[]{:S(2)}) async-start(bf16[8,4,16,8,128]{4,3,2,1,0:T(8,128)(2,1)} %broadcast_in_dim.12), calls=%async_computation | async-start | bytes 2097152 | tf_op jit(solution)/shard_map/all_to_all | solution.py:26
  34.6 5.5 %copy-start.3 = (f32[1024]{0:T(1024)S(1)}, f32[1024]{0:T(1024)}, u32[]{:S(2)}) copy-start(f32[1024]{0:T(1024)} %param.7) | copy-start | bytes 12292
  47.8 3.7 %copy-start = (f32[16,8,128]{2,1,0:T(8,128)S(1)}, f32[16,8,128]{2,1,0:T(8,128)}, u32[]{:S(2)}) copy-start(f32[16,8,128]{2,1,0:T(8,128)} %param.5) | copy-start | bytes 196612
  47.8 24.0 %all-to-all-start.1 = ((f32[8,40,1025]{2,1,0:T(8,128)}), f32[8,40,1025]{2,1,0:T(8,128)S(1)}, u32[]{:S(2)}, u32[]{:S(2)}) async-start(f32[8,40,1025]{2,1,0:T(8,128)} %broadcast_in_dim.13), calls=%async_computation.1 | async-start | bytes 2949120 | tf_op jit(solution)/shard_map/all_to_all | solution.py:26
  51.5 48.2 %copy-start.1 = (f32[16,8,128]{2,1,0:T(8,128)S(1)}, f32[16,8,128]{2,1,0:T(8,128)}, u32[]{:S(2)}) copy-start(f32[16,8,128]{2,1,0:T(8,128)} %param.6) | copy-start | bytes 196612
  51.5 34.5 %collective-permute-start.8 = (f32[1,8,128]{2,1,0:T(8,128)S(1)}, f32[1,8,128]{2,1,0:T(8,128)S(1)}, u32[]{:S(2)}, u32[]{:S(2)}) collective-permute-start(f32[1,8,128]{2,1,0:T(8,128)S(1)} %get-tuple-element.21), channel_id=1, source_target_pairs={{1,0},{2,1},{3,2},{4,3},{5,4},{6,5},{7,6},{9,8},{10,9},{11,10},{12... | collective-permute-start | bytes 12296 | tf_op jit(solution)/shard_map/ppermute | solution.py:56
  52.8 38.3 %collective-permute-start.9 = (f32[1,8,128]{2,1,0:T(8,128)S(1)}, f32[1,8,128]{2,1,0:T(8,128)S(1)}, u32[]{:S(2)}, u32[]{:S(2)}) collective-permute-start(f32[1,8,128]{2,1,0:T(8,128)S(1)} %get-tuple-element.22), channel_id=1, source_target_pairs={{0,1},{1,2},{2,3},{3,4},{4,5},{5,6},{6,7},{8,9},{9,10},{10,11},{11... | collective-permute-start | bytes 12296 | tf_op jit(solution)/shard_map/ppermute | solution.py:55
  75.5 24.2 %collective-permute-start.3 = (f32[16,8,128]{2,1,0:T(8,128)S(1)}, f32[16,8,128]{2,1,0:T(8,128)S(1)}, u32[]{:S(2)}, u32[]{:S(2)}) collective-permute-start(f32[16,8,128]{2,1,0:T(8,128)S(1)} %bitcast.108), channel_id=1, source_target_pairs={{8,0},{16,8},{24,16},{32,24},{40,32},{48,40},{56,48},{64,56},{72,6... | collective-permute-start | bytes 196616 | tf_op jit(solution)/shard_map/ppermute | solution.py:15
  78.2 21.5 %collective-permute-start.4 = (f32[16,8,128]{2,1,0:T(8,128)S(1)}, f32[16,8,128]{2,1,0:T(8,128)S(1)}, u32[]{:S(2)}, u32[]{:S(2)}) collective-permute-start(f32[16,8,128]{2,1,0:T(8,128)S(1)} %bitcast.110), channel_id=1, source_target_pairs={{16,0},{24,8},{32,16},{40,24},{48,32},{56,40},{64,48},{72,56},{80,... | collective-permute-start | bytes 196616 | tf_op jit(solution)/shard_map/ppermute | solution.py:15
  80.7 19.0 %collective-permute-start.5 = (f32[16,8,128]{2,1,0:T(8,128)S(1)}, f32[16,8,128]{2,1,0:T(8,128)S(1)}, u32[]{:S(2)}, u32[]{:S(2)}) collective-permute-start(f32[16,8,128]{2,1,0:T(8,128)S(1)} %bitcast.112), channel_id=1, source_target_pairs={{24,0},{32,8},{40,16},{48,24},{56,32},{64,40},{72,48},{80,56},{88,... | collective-permute-start | bytes 196616 | tf_op jit(solution)/shard_map/ppermute | solution.py:15
  86.1 7.0 %collective-permute-start.6 = (f32[16,1,128]{2,1,0:T(1,128)S(1)}, f32[16,1,128]{2,1,0:T(1,128)S(1)}, u32[]{:S(2)}, u32[]{:S(2)}) collective-permute-start(f32[16,1,128]{2,1,0:T(1,128)S(1)} %get-tuple-element.24), channel_id=1, source_target_pairs={{0,8},{8,16},{16,24},{24,32},{32,40},{40,48},{48,56},{56,64},{64,7... | collective-permute-start | bytes 24584 | tf_op jit(solution)/shard_map/ppermute | solution.py:55
  91.1 8.6 %collective-permute-start.7 = (f32[16,1,128]{2,1,0:T(1,128)S(1)}, f32[16,1,128]{2,1,0:T(1,128)S(1)}, u32[]{:S(2)}, u32[]{:S(2)}) collective-permute-start(f32[16,1,128]{2,1,0:T(1,128)S(1)} %get-tuple-element.23), channel_id=1, source_target_pairs={{8,0},{16,8},{24,16},{32,24},{40,32},{48,40},{56,48},{64,56},{72,6... | collective-permute-start | bytes 24584 | tf_op jit(solution)/shard_map/ppermute | solution.py:56
  99.9 5.8 %collective-permute-start.10 = (bf16[16,8,128]{2,1,0:T(8,128)(2,1)S(1)}, bf16[16,8,128]{2,1,0:T(8,128)(2,1)S(1)}, u32[]{:S(2)}, u32[]{:S(2)}) collective-permute-start(bf16[16,8,128]{2,1,0:T(8,128)(2,1)S(1)} %get-tuple-element.5), channel_id=1, source_target_pairs={{0,8},{8,16},{16,24},{24,32},{32,40},{40,48},{48,56},{56,64},{64,7... | collective-permute-start | bytes 98312 | tf_op jit(solution)/shard_map/ppermute | solution.py:15
  101.8 4.7 %collective-permute-start.11 = (bf16[16,8,128]{2,1,0:T(8,128)(2,1)S(1)}, bf16[16,8,128]{2,1,0:T(8,128)(2,1)S(1)}, u32[]{:S(2)}, u32[]{:S(2)}) collective-permute-start(bf16[16,8,128]{2,1,0:T(8,128)(2,1)S(1)} %get-tuple-element.5), channel_id=1, source_target_pairs={{0,16},{8,24},{16,32},{24,40},{32,48},{40,56},{48,64},{56,72},{64,... | collective-permute-start | bytes 98312 | tf_op jit(solution)/shard_map/ppermute | solution.py:15
  103.7 5.9 %collective-permute-start.12 = (bf16[16,8,128]{2,1,0:T(8,128)(2,1)S(1)}, bf16[16,8,128]{2,1,0:T(8,128)(2,1)S(1)}, u32[]{:S(2)}, u32[]{:S(2)}) collective-permute-start(bf16[16,8,128]{2,1,0:T(8,128)(2,1)S(1)} %get-tuple-element.5), channel_id=1, source_target_pairs={{0,24},{8,32},{16,40},{24,48},{32,56},{40,64},{48,72},{56,80},{64,... | collective-permute-start | bytes 98312 | tf_op jit(solution)/shard_map/ppermute | solution.py:15
  141.3 23.9 %all-to-all-start.3 = ((f32[8,40,1025]{2,1,0:T(8,128)}), f32[8,40,1025]{2,1,0:T(8,128)S(1)}, u32[]{:S(2)}, u32[]{:S(2)}) async-start(f32[8,40,1025]{2,1,0:T(8,128)} %broadcast_in_dim.17), calls=%async_computation.3 | async-start | bytes 2949120 | tf_op jit(solution)/shard_map/all_to_all | solution.py:26
  144.9 32.3 %collective-permute-start.18 = (f32[1,8,128]{2,1,0:T(8,128)S(1)}, f32[1,8,128]{2,1,0:T(8,128)S(1)}, u32[]{:S(2)}, u32[]{:S(2)}) collective-permute-start(f32[1,8,128]{2,1,0:T(8,128)S(1)} %get-tuple-element.17), channel_id=1, source_target_pairs={{1,0},{2,1},{3,2},{4,3},{5,4},{6,5},{7,6},{9,8},{10,9},{11,10},{12... | collective-permute-start | bytes 12296 | tf_op jit(solution)/shard_map/ppermute | solution.py:56
  146.2 36.8 %collective-permute-start.19 = (f32[1,8,128]{2,1,0:T(8,128)S(1)}, f32[1,8,128]{2,1,0:T(8,128)S(1)}, u32[]{:S(2)}, u32[]{:S(2)}) collective-permute-start(f32[1,8,128]{2,1,0:T(8,128)S(1)} %get-tuple-element.18), channel_id=1, source_target_pairs={{0,1},{1,2},{2,3},{3,4},{4,5},{5,6},{6,7},{8,9},{9,10},{10,11},{11... | collective-permute-start | bytes 12296 | tf_op jit(solution)/shard_map/ppermute | solution.py:55
  168.9 22.8 %collective-permute-start.13 = (f32[16,8,128]{2,1,0:T(8,128)S(1)}, f32[16,8,128]{2,1,0:T(8,128)S(1)}, u32[]{:S(2)}, u32[]{:S(2)}) collective-permute-start(f32[16,8,128]{2,1,0:T(8,128)S(1)} %bitcast.109), channel_id=1, source_target_pairs={{8,0},{16,8},{24,16},{32,24},{40,32},{48,40},{56,48},{64,56},{72,6... | collective-permute-start | bytes 196616 | tf_op jit(solution)/shard_map/ppermute | solution.py:15
  171.6 20.0 %collective-permute-start.14 = (f32[16,8,128]{2,1,0:T(8,128)S(1)}, f32[16,8,128]{2,1,0:T(8,128)S(1)}, u32[]{:S(2)}, u32[]{:S(2)}) collective-permute-start(f32[16,8,128]{2,1,0:T(8,128)S(1)} %bitcast.111), channel_id=1, source_target_pairs={{16,0},{24,8},{32,16},{40,24},{48,32},{56,40},{64,48},{72,56},{80,... | collective-permute-start | bytes 196616 | tf_op jit(solution)/shard_map/ppermute | solution.py:15
  174.1 17.6 %collective-permute-start.15 = (f32[16,8,128]{2,1,0:T(8,128)S(1)}, f32[16,8,128]{2,1,0:T(8,128)S(1)}, u32[]{:S(2)}, u32[]{:S(2)}) collective-permute-start(f32[16,8,128]{2,1,0:T(8,128)S(1)} %bitcast.113), channel_id=1, source_target_pairs={{24,0},{32,8},{40,16},{48,24},{56,32},{64,40},{72,48},{80,56},{88,... | collective-permute-start | bytes 196616 | tf_op jit(solution)/shard_map/ppermute | solution.py:15
  177.3 7.7 %collective-permute-start.16 = (f32[16,1,128]{2,1,0:T(1,128)S(1)}, f32[16,1,128]{2,1,0:T(1,128)S(1)}, u32[]{:S(2)}, u32[]{:S(2)}) collective-permute-start(f32[16,1,128]{2,1,0:T(1,128)S(1)} %get-tuple-element.20), channel_id=1, source_target_pairs={{0,8},{8,16},{16,24},{24,32},{32,40},{40,48},{48,56},{56,64},{64,7... | collective-permute-start | bytes 24584 | tf_op jit(solution)/shard_map/ppermute | solution.py:55
  183.0 8.6 %collective-permute-start.17 = (f32[16,1,128]{2,1,0:T(1,128)S(1)}, f32[16,1,128]{2,1,0:T(1,128)S(1)}, u32[]{:S(2)}, u32[]{:S(2)}) collective-permute-start(f32[16,1,128]{2,1,0:T(1,128)S(1)} %get-tuple-element.19), channel_id=1, source_target_pairs={{8,0},{16,8},{24,16},{32,24},{40,32},{48,40},{56,48},{64,56},{72,6... | collective-permute-start | bytes 24584 | tf_op jit(solution)/shard_map/ppermute | solution.py:56
where the time goes:
time: 193 us; the launch traced here: 192 us
  starting transfers between devices  71.1 us (37%)
  waiting for transfers between devices  63.6 us (33%)
  matrix products  22.5 us (12%)
  blocking collectives  17.2 us (9%)
  other arithmetic  9.99 us (5%)
  local copies, waits for them, and re-layouts  7.53 us (4%)
    all_to_all x3, waiting for transfers between devices, sent_to_all(): lax.all_to_all(jnp.broadcast_to(value[None], (length, *value.shape)), axi...  45.5 us
    ppermute x12, starting transfers between devices, passed_along(): return lax.ppermute(block, axis, route)  33.9 us
    ppermute x4, starting transfers between devices, padded_2(): lax.ppermute(last, axis, up)  18.9 us
    all_to_all x1, blocking collectives, sent_to_all(): lax.all_to_all(jnp.broadcast_to(value[None], (length, *value.shape)), axi...  17.2 us
    ppermute x4, waiting for transfers between devices, padded_2(): lax.ppermute(first, axis, [(b, a) for a, b in up])  13.3 us
    all_to_all x3, starting transfers between devices, sent_to_all(): lax.all_to_all(jnp.broadcast_to(value[None], (length, *value.shape)), axi...  11.9 us
    dot_general x2, matrix products, local(): jnp.einsum('tok,tk->to', footprint, gathered_blocks, preferred_element_ty...  11 us
    dot_general x2, matrix products, local(): jnp.einsum('tok,to->tk', footprint, spread, preferred_element_type=jnp.fl...  10.9 us
  transfers between devices with their start and end apart: 23, of which 8 were waited for; matrix products, arithmetic and copies ran while one was open for 4% of the time, Pallas kernels for 0%

commit v1 on v0

v1 whole, which is shorter than its diff:
```python
import functools

import jax
import jax.numpy as jnp
from jax import lax
from jax.experimental import pallas as pl
from jax.experimental.pallas import tpu as pltpu
from jax.sharding import PartitionSpec as P

LAG = 4
ITERS = 2
SLOTS = 48
SPREAD = 64
ROWS = 16
HOURS = 8
CELLS = 128
OBS = 128
NOB = 8
GROUP = 16
MESH = pl.DeviceIdType.MESH
HIGHEST = lax.Precision.HIGHEST


def take(ref, sem):
    pltpu.make_async_copy(ref, ref, sem).wait()


def dot(a, b, dims, precision=None):
    return lax.dot_general(
        a, b, (dims, ((), ())), precision=precision, preferred_element_type=jnp.float32
    )


def kernel(
    n_tm,
    n_region,
    tiles,
    flux_ref,
    penalty_ref,
    observed_ref,
    index_ref,
    footprint_ref,
    out_ref,
    foot,
    flux,
    low,
    window,
    blocks,
    slots,
    terms,
    all_terms,
    sums,
    parts,
    edges,
    edge_rows,
    edge_hours,
    index_pad,
    picks,
    pick,
    pick_t,
    foot_sem,
    pick_sem,
    send_sem,
    recv_sem,
    edge_send,
    edge_recv,
):
    w = lax.axis_index("tm")
    r = lax.axis_index("region")
    later = [lax.rem(w + l, n_tm) for l in range(LAG)]
    earlier = [lax.rem(w + n_tm - l, n_tm) for l in range(LAG)]
    region = [lax.rem(r + k, n_region) for k in range(n_region)]
    others = [(l, k) for l in reversed(range(LAG)) for k in range(n_region) if (l, k) != (0, 0)]
    table_rows = LAG * n_region * ROWS

    load = pltpu.make_async_copy(footprint_ref, foot, foot_sem)
    load.start()

    barrier = pltpu.get_barrier_semaphore()
    for l, k in others:
        pl.semaphore_signal(
            barrier, inc=1, device_id={"tm": earlier[l], "region": region[k]}, device_id_type=MESH
        )

    def send(src, dst, sent, received, tm, reg):
        pltpu.make_async_remote_copy(
            src_ref=src,
            dst_ref=dst,
            send_sem=sent,
            recv_sem=received,
            device_id={"tm": tm, "region": reg},
            device_id_type=MESH,
        ).start()

    index_pad[...] = jnp.zeros_like(index_pad)
    index_pad[0:4, 0:tiles] = index_ref[...]
    entries = index_pad[...]
    lag = entries[1:2, :]
    usable = (entries[3:4, :] == 1) & (lag <= w)
    mine = jnp.where(usable, lag * (n_region * ROWS) + entries[2:3, :], -1)
    picks[r] = jnp.broadcast_to(mine, (8, 128))
    for h in range(HOURS):
        flux[0, h] = flux_ref[:, h, :]
        low[0, h] = flux[0, h].astype(jnp.bfloat16)
    all_terms[...] = jnp.zeros_like(all_terms)

    pl.semaphore_wait(barrier, len(others))

    for i in range(ITERS):
        for l, k in others:
            send(
                low.at[i, region[k]],
                window.at[i, l * n_region + r],
                send_sem.at[i, 0],
                recv_sem.at[i, 0],
                later[l],
                region[k],
            )
        window[i, r] = low[i, r]
        if i == 0:
            for k in range(1, n_region):
                send(picks.at[r], picks.at[r], pick_sem.at[0], pick_sem.at[1], w, region[k])
        edges[i, 0] = flux[i, :, 0, :]
        edges[i, 1] = flux[i, :, ROWS - 1, :]
        send(
            edges.at[i, 0], edge_rows.at[i, 1],
            edge_send.at[i, 0], edge_recv.at[i, 0], w, region[n_region - 1],
        )
        send(
            edges.at[i, 1], edge_rows.at[i, 0],
            edge_send.at[i, 1], edge_recv.at[i, 1], w, region[1],
        )
        send(
            flux.at[i, HOURS - 1], edge_hours.at[i, 0],
            edge_send.at[i, 2], edge_recv.at[i, 2], later[1], r,
        )
        if i == 0:
            take(picks.at[0 : n_region - 1], pick_sem.at[1])
            rows = picks[:, 0, :]
            columns = jnp.transpose(jnp.concatenate([rows] * 16, axis=0))
            across = lax.broadcasted_iota(jnp.int32, (SLOTS, table_rows), 1)
            for d in range(n_region):
                chosen = columns[0:SLOTS, d : d + 1] == across
                pick[d * SLOTS : (d + 1) * SLOTS, :] = chosen.astype(jnp.float32).astype(jnp.bfloat16)
            lane = lax.broadcasted_iota(jnp.int32, (1, 128), 1)
            moved = pltpu.roll(rows, SPREAD, 1)
            down = lax.broadcasted_iota(jnp.int32, (table_rows, 128), 0)
            for d in range(0, n_region, 2):
                pair = jnp.where(lane < SPREAD, rows[d : d + 1], moved[d + 1 : d + 2])
                chosen = down == pair
                pick_t[:, d * SPREAD : (d + 2) * SPREAD] = chosen.astype(jnp.float32).astype(
                    jnp.bfloat16
                )
        take(window.at[i, 0 : len(others)], recv_sem.at[i, 0])
        send(
            flux.at[i, 0], edge_hours.at[i, 1],
            edge_send.at[i, 3], edge_recv.at[i, 3], earlier[1], r,
        )

        table = window[i].reshape(table_rows, CELLS)
        blocks[i] = (
            dot(pick[...], table, ((1,), (0,)))
            .astype(jnp.bfloat16)
            .reshape(n_region, SLOTS, CELLS)
        )
        for k in range(1, n_region):
            send(
                blocks.at[i, region[k]], slots.at[i, r],
                send_sem.at[i, 1], recv_sem.at[i, 1], w, region[k],
            )
        slots[i, r] = blocks[i, r]
        if i == 0:
            load.wait()
        take(slots.at[i, 0 : n_region - 1], recv_sem.at[i, 1])

        down = lax.broadcasted_iota(jnp.int32, (GROUP, OBS), 0)
        x = jnp.concatenate([slots[i, h] for h in range(HOURS)], axis=1)
        products = []
        for first in range(0, SLOTS, GROUP):
            x_group = x[first : first + GROUP, :]
            total = jnp.zeros((GROUP, OBS), jnp.float32)
            for t in range(first, min(first + GROUP, tiles), 2):
                both = dot(x_group, foot[t * OBS : (t + 2) * OBS, :], ((1,), (1,)))
                total = jnp.where(down == t - first, both[:, :OBS], total)
                total = jnp.where(down == t + 1 - first, both[:, OBS:], total)
            products.append(total)
        products = jnp.concatenate(products, axis=0)
        row_block = index_pad[0:1, 0:SLOTS]
        selector = (lax.broadcasted_iota(jnp.int32, (NOB, SLOTS), 0) == row_block).astype(jnp.float32)
        predicted = dot(selector, products, ((1,), (0,)), HIGHEST)
        residual = (predicted - observed_ref[...]).astype(jnp.bfloat16).astype(jnp.float32)

        spread = jnp.zeros((SLOTS, OBS), jnp.float32)
        block_of = jnp.transpose(index_pad[...])[0:SLOTS, 0:1]
        for b in range(NOB):
            spread = jnp.where(block_of == b, residual[b : b + 1, :], spread)
        lefts = []
        for first in range(0, SLOTS, GROUP):
            part = spread[first : first + GROUP, :]
            lefts.append(
                jnp.concatenate(
                    [
                        jnp.where(down == t - first, part, 0.0)
                        for t in range(first, min(first + GROUP, tiles))
                    ],
                    axis=1,
                ).astype(jnp.bfloat16)
            )
        for h in range(0, HOURS, 2):
            for g, first in enumerate(range(0, SLOTS, GROUP)):
                last = min(first + GROUP, tiles)
                both = dot(
                    lefts[g],
                    foot[first * OBS : last * OBS, h * CELLS : (h + 2) * CELLS],
                    ((1,), (0,)),
                ).astype(jnp.bfloat16)
                terms[i, h, first : first + GROUP, :] = both[:, :CELLS]
                terms[i, h + 1, first : first + GROUP, :] = both[:, CELLS:]
        for k in range(1, n_region):
            send(
                terms.at[i, region[k]], all_terms.at[i, r, 0:SLOTS],
                send_sem.at[i, 2], recv_sem.at[i, 2], w, region[k],
            )
        all_terms[i, r, 0:SLOTS] = terms[i, r]
        take(all_terms.at[i, 0 : n_region - 1, 0:SLOTS], recv_sem.at[i, 2])

        received = all_terms[i].reshape(n_region * SPREAD, CELLS)
        sums[i] = (
            dot(pick_t[...], received, ((1,), (0,)))
            .astype(jnp.bfloat16)
            .reshape(LAG * n_region, ROWS, CELLS)
        )
        for l, k in others:
            send(
                sums.at[i, l * n_region + region[k]],
                parts.at[i, l * n_region + r],
                send_sem.at[i, 3],
                recv_sem.at[i, 3],
                earlier[l],
                region[k],
            )
        parts[i, r] = sums[i, r]
        for e in range(2):
            take(edge_rows.at[i, e], edge_recv.at[i, e])
            take(edge_hours.at[i, e], edge_recv.at[i, 2 + e])
        take(parts.at[i, 0 : len(others)], recv_sem.at[i, 3])

        row_low = jnp.where(r > 0, edge_rows[i, 0], 0.0)
        row_high = jnp.where(r < n_region - 1, edge_rows[i, 1], 0.0)
        hour_low = jnp.where(w > 0, edge_hours[i, 0], 0.0)
        hour_high = jnp.where(w < n_tm - 1, edge_hours[i, 1], 0.0)
        cell = lax.broadcasted_iota(jnp.int32, (ROWS, CELLS), 1)
        planes = [hour_low] + [flux[i, h] for h in range(HOURS)] + [hour_high]
        for h in range(HOURS):
            here = planes[h + 1]
            adjoint = parts[i, h].astype(jnp.float32)
            for l in range(1, LAG):
                adjoint = adjoint + parts[i, l * n_region + h].astype(jnp.float32)
            neighbours = jnp.concatenate([here[1:], row_high[h : h + 1]], axis=0)
            neighbours = neighbours + jnp.concatenate([row_low[h : h + 1], here[:-1]], axis=0)
            neighbours = neighbours + planes[h + 2] + planes[h]
            neighbours = neighbours + jnp.where(cell < CELLS - 1, pltpu.roll(here, CELLS - 1, 1), 0.0)
            neighbours = neighbours + jnp.where(cell > 0, pltpu.roll(here, 1, 1), 0.0)
            laplace = 6.0 * here - neighbours
            stepped = here - 0.5 * (adjoint + 0.2 * laplace)
            cutoff = 0.5 * penalty_ref[:, h, :]
            new = stepped - jnp.clip(stepped, -cutoff, cutoff)
            if i < ITERS - 1:
                flux[i + 1, h] = new
                low[i + 1, h] = new.astype(jnp.bfloat16)
            else:
                out_ref[:, h, :] = new

    take(picks.at[0 : n_region - 1], pick_sem.at[0])
    for i in range(ITERS):
        take(window.at[i, 0 : len(others)], send_sem.at[i, 0])
        take(slots.at[i, 0 : n_region - 1], send_sem.at[i, 1])
        take(terms.at[i, 0 : n_region - 1], send_sem.at[i, 2])
        take(parts.at[i, 0 : len(others)], send_sem.at[i, 3])
        for e in range(2):
            take(edge_rows.at[i, e], edge_send.at[i, e])
            take(edge_hours.at[i, e], edge_send.at[i, 2 + e])


def local(flux_init, penalty, observed, footprint, tile_index):
    n_tm, n_region = lax.axis_size("tm"), lax.axis_size("region")
    tiles = tile_index.shape[0]
    in_vmem = pl.BlockSpec(memory_space=pltpu.VMEM)
    table = LAG * n_region
    half, full = jnp.bfloat16, jnp.float32
    dma = pltpu.SemaphoreType.DMA
    return pl.pallas_call(
        functools.partial(kernel, n_tm, n_region, tiles),
        out_shape=jax.ShapeDtypeStruct(flux_init.shape, full),
        in_specs=[in_vmem] * 4 + [pl.BlockSpec(memory_space=pl.ANY)],
        out_specs=in_vmem,
        scratch_shapes=[
            pltpu.VMEM((tiles * OBS, HOURS * CELLS), half),
            pltpu.VMEM((ITERS, HOURS, ROWS, CELLS), full),
            pltpu.VMEM((ITERS, HOURS, ROWS, CELLS), half),
            pltpu.VMEM((ITERS, table, ROWS, CELLS), half),
            pltpu.VMEM((ITERS, n_region, SLOTS, CELLS), half),
            pltpu.VMEM((ITERS, n_region, SLOTS, CELLS), half),
            pltpu.VMEM((ITERS, n_region, SLOTS, CELLS), half),
            pltpu.VMEM((ITERS, n_region, SPREAD, CELLS), half),
            pltpu.VMEM((ITERS, table, ROWS, CELLS), half),
            pltpu.VMEM((ITERS, table, ROWS, CELLS), half),
            pltpu.VMEM((ITERS, 2, HOURS, CELLS), full),
            pltpu.VMEM((ITERS, 2, HOURS, CELLS), full),
            pltpu.VMEM((ITERS, 2, ROWS, CELLS), full),
            pltpu.VMEM((128, 128), jnp.int32),
            pltpu.VMEM((n_region, 8, 128), jnp.int32),
            pltpu.VMEM((n_region * SLOTS, table * ROWS), half),
            pltpu.VMEM((table * ROWS, n_region * SPREAD), half),
            dma,
            dma((2,)),
            dma((ITERS, 4)),
            dma((ITERS, 4)),
            dma((ITERS, 4)),
            dma((ITERS, 4)),
        ],
        compiler_params=pltpu.CompilerParams(
            collective_id=0, has_side_effects=True, vmem_limit_bytes=60 * 2**20
        ),
        cost_estimate=pl.CostEstimate(
            flops=8 * footprint.size, bytes_accessed=2 * footprint.size, transcendentals=0
        ),
    )(
        flux_init,
        penalty,
        observed.reshape(NOB, OBS),
        tile_index.T,
        footprint.reshape(tiles * OBS, HOURS * CELLS),
    )


def solution(mesh):
    in_specs = (
        P("region", "tm", None),
        P("region", "tm", None),
        P(("tm", "region")),
        P(("tm", "region"), None, None),
        P(("tm", "region"), None),
    )
    out_specs = P("region", "tm", None)
    return jax.shard_map(local, mesh=mesh, in_specs=in_specs, out_specs=out_specs, check_vma=False)
```

time: 193 us -> 65 us (0.34)
  the two profiles are of different devices: /device:TPU:225 before, /device:TPU:1 now
where the time goes in v1:
time: 65 us; the launch traced here: 64.8 us
  Pallas kernels  63.3 us (97%)
  local copies, waits for them, and re-layouts  1.47 us (2%)
    pallas_call x1, Pallas kernels, local(): pl.pallas_call(functools.partial(kernel, n_tm, n_region, tiles), out_shap...  63.3 us
    unnamed x1, local copies, waits for them, and re-layouts  1.47 us

profile of v1, /device:TPU:1, one launch (start us, length us, event | category | flops | bytes accessed | tf_op | source)
XLA Modules:
  0.0 64.8 jit_solution(12182433059305244661)
XLA Ops:
  0.0 63.3 %shard_map.55 = f32[16,8,128]{2,1,0:T(8,128)} custom-call(f32[16,8,128]{2,1,0:T(8,128)} %flux_ref.1, f32[16,8,128]{2,1,0:T(8,128)} %penalty_ref.1, f32[8,128]{1,0:T(8,128)} %bitcast.4, s32[4,40]{1,0:T(4,128)} %bitcast.5, bf16[5120,1024]{1,0:T(8,128)(2,1)} %bitcast.3), custom_call_target="tpu_custom_call" | custom-call | flops 41943040 | bytes 10485760 | tf_op jit(solution)/shard_map/pallas_call | solution.py:292
  63.3 1.5 %copy.7 = f32[16,8,128]{2,1,0:T(8,128)} copy(f32[16,8,128]{2,1,0:T(8,128)} %shard_map.55) | data formatting | bytes 131072

commit v2 on v1

--- a/solution.py
+++ b/solution.py
@@ -42,6 +42,7 @@
     footprint_ref,
     out_ref,
     foot,
+    foot_t,
     flux,
     low,
     window,
@@ -62,6 +63,7 @@
     pick_sem,
     send_sem,
     recv_sem,
+    slot_recv,
     edge_send,
     edge_recv,
 ):
@@ -72,6 +74,11 @@
     region = [lax.rem(r + k, n_region) for k in range(n_region)]
     others = [(l, k) for l in reversed(range(LAG)) for k in range(n_region) if (l, k) != (0, 0)]
     table_rows = LAG * n_region * ROWS
+    own = r // 2
+    flip = own + 1 - 2 * lax.rem(own, 2)
+    pairs = [own, flip, lax.rem(own + 2, 4), lax.rem(flip + 2, 4)]
+    partner = r + 1 - 2 * lax.rem(r, 2)
+    near_first = [partner] + [2 * q + e for q in pairs[1:] for e in range(2)]
 
     load = pltpu.make_async_copy(footprint_ref, foot, foot_sem)
     load.start()
@@ -135,6 +142,9 @@
             edge_send.at[i, 2], edge_recv.at[i, 2], later[1], r,
         )
         if i == 0:
+            load.wait()
+            for t in range(tiles):
+                foot_t[:, t * OBS : (t + 1) * OBS] = jnp.transpose(foot[t * OBS : (t + 1) * OBS, :])
             take(picks.at[0 : n_region - 1], pick_sem.at[1])
             rows = picks[:, 0, :]
             columns = jnp.transpose(jnp.concatenate([rows] * 16, axis=0))
@@ -163,27 +173,29 @@
             .astype(jnp.bfloat16)
             .reshape(n_region, SLOTS, CELLS)
         )
-        for k in range(1, n_region):
+        for reg in reversed(near_first):
             send(
-                blocks.at[i, region[k]], slots.at[i, r],
-                send_sem.at[i, 1], recv_sem.at[i, 1], w, region[k],
+                blocks.at[i, reg], slots.at[i, r],
+                send_sem.at[i, 1], slot_recv.at[i, r], w, reg,
             )
         slots[i, r] = blocks[i, r]
-        if i == 0:
-            load.wait()
-        take(slots.at[i, 0 : n_region - 1], recv_sem.at[i, 1])
 
         down = lax.broadcasted_iota(jnp.int32, (GROUP, OBS), 0)
-        x = jnp.concatenate([slots[i, h] for h in range(HOURS)], axis=1)
-        products = []
-        for first in range(0, SLOTS, GROUP):
-            x_group = x[first : first + GROUP, :]
-            total = jnp.zeros((GROUP, OBS), jnp.float32)
-            for t in range(first, min(first + GROUP, tiles), 2):
-                both = dot(x_group, foot[t * OBS : (t + 2) * OBS, :], ((1,), (1,)))
-                total = jnp.where(down == t - first, both[:, :OBS], total)
-                total = jnp.where(down == t + 1 - first, both[:, OBS:], total)
-            products.append(total)
+        groups = [(first, min(first + GROUP, tiles)) for first in range(0, SLOTS, GROUP)]
+        products = [jnp.zeros((GROUP, OBS), jnp.float32) for _ in groups]
+        for step, q in enumerate(pairs):
+            for reg in [2 * q, 2 * q + 1] if step else [partner]:
+                take(slots.at[i, reg], slot_recv.at[i, reg])
+            x = jnp.concatenate([slots[i, 2 * q], slots[i, 2 * q + 1]], axis=1)
+            cells = pl.ds(pl.multiple_of(q * 2 * CELLS, 2 * CELLS), 2 * CELLS)
+            for g, (first, last) in enumerate(groups):
+                x_group = x[first : first + GROUP, :]
+                total = jnp.zeros((GROUP, OBS), jnp.float32)
+                for t in range(first, last, 2):
+                    both = dot(x_group, foot_t[cells, t * OBS : (t + 2) * OBS], ((1,), (0,)))
+                    total = jnp.where(down == t - first, both[:, :OBS], total)
+                    total = jnp.where(down == t + 1 - first, both[:, OBS:], total)
+                products[g] = products[g] + total
         products = jnp.concatenate(products, axis=0)
         row_block = index_pad[0:1, 0:SLOTS]
         selector = (lax.broadcasted_iota(jnp.int32, (NOB, SLOTS), 0) == row_block).astype(jnp.float32)
@@ -206,21 +218,19 @@
                     axis=1,
                 ).astype(jnp.bfloat16)
             )
-        for h in range(0, HOURS, 2):
-            for g, first in enumerate(range(0, SLOTS, GROUP)):
-                last = min(first + GROUP, tiles)
+        for q in reversed(pairs):
+            cells = pl.ds(pl.multiple_of(q * 2 * CELLS, 2 * CELLS), 2 * CELLS)
+            for g, (first, last) in enumerate(groups):
                 both = dot(
-                    lefts[g],
-                    foot[first * OBS : last * OBS, h * CELLS : (h + 2) * CELLS],
-                    ((1,), (0,)),
+                    lefts[g], foot[first * OBS : last * OBS, cells], ((1,), (0,))
                 ).astype(jnp.bfloat16)
-                terms[i, h, first : first + GROUP, :] = both[:, :CELLS]
-                terms[i, h + 1, first : first + GROUP, :] = both[:, CELLS:]
-        for k in range(1, n_region):
-            send(
-                terms.at[i, region[k]], all_terms.at[i, r, 0:SLOTS],
-                send_sem.at[i, 2], recv_sem.at[i, 2], w, region[k],
-            )
+                terms[i, 2 * q, first : first + GROUP, :] = both[:, :CELLS]
+                terms[i, 2 * q + 1, first : first + GROUP, :] = both[:, CELLS:]
+            for reg in [2 * q, 2 * q + 1] if q is not own else [partner]:
+                send(
+                    terms.at[i, reg], all_terms.at[i, r, 0:SLOTS],
+                    send_sem.at[i, 2], recv_sem.at[i, 2], w, reg,
+                )
         all_terms[i, r, 0:SLOTS] = terms[i, r]
         take(all_terms.at[i, 0 : n_region - 1, 0:SLOTS], recv_sem.at[i, 2])
 
@@ -296,6 +306,7 @@
         out_specs=in_vmem,
         scratch_shapes=[
             pltpu.VMEM((tiles * OBS, HOURS * CELLS), half),
+            pltpu.VMEM((HOURS * CELLS, tiles * OBS), half),
             pltpu.VMEM((ITERS, HOURS, ROWS, CELLS), full),
             pltpu.VMEM((ITERS, HOURS, ROWS, CELLS), half),
             pltpu.VMEM((ITERS, table, ROWS, CELLS), half),
@@ -316,11 +327,12 @@
             dma((2,)),
             dma((ITERS, 4)),
             dma((ITERS, 4)),
+            dma((ITERS, n_region)),
             dma((ITERS, 4)),
             dma((ITERS, 4)),
         ],
         compiler_params=pltpu.CompilerParams(
-            collective_id=0, has_side_effects=True, vmem_limit_bytes=60 * 2**20
+            collective_id=0, has_side_effects=True, vmem_limit_bytes=55 * 2**20
         ),
         cost_estimate=pl.CostEstimate(
             flops=8 * footprint.size, bytes_accessed=2 * footprint.size, transcendentals=0

time: 65 us -> 60 us (0.923)
  Pallas kernels: 63.3 us -> 58.3 us
    pallas_call x1, Pallas kernels: 63.3 us -> 58.3 us  [local(): pl.pallas_call(functools.partial(kernel, n_tm, n_region, tiles), out_shap...]
where the time goes in v2:
time: 60 us; the launch traced here: 59.8 us
  Pallas kernels  58.3 us (97%)
  local copies, waits for them, and re-layouts  1.47 us (2%)
    pallas_call x1, Pallas kernels, local(): pl.pallas_call(functools.partial(kernel, n_tm, n_region, tiles), out_shap...  58.3 us
    unnamed x1, local copies, waits for them, and re-layouts  1.47 us

profile of v2, /device:TPU:1, one launch (start us, length us, event | category | flops | bytes accessed | tf_op | source)
XLA Modules:
  0.0 59.8 jit_solution(2384679263122901306)
XLA Ops:
  0.0 58.3 %shard_map.55 = f32[16,8,128]{2,1,0:T(8,128)} custom-call(f32[16,8,128]{2,1,0:T(8,128)} %flux_ref.1, f32[16,8,128]{2,1,0:T(8,128)} %penalty_ref.1, f32[8,128]{1,0:T(8,128)} %bitcast.4, s32[4,40]{1,0:T(4,128)} %bitcast.5, bf16[5120,1024]{1,0:T(8,128)(2,1)} %bitcast.3), custom_call_target="tpu_custom_call" | custom-call | flops 41943040 | bytes 10485760 | tf_op jit(solution)/shard_map/pallas_call | solution.py:302
  58.3 1.5 %copy.7 = f32[16,8,128]{2,1,0:T(8,128)} copy(f32[16,8,128]{2,1,0:T(8,128)} %shard_map.55) | data formatting | bytes 131072

commit v3 on v2

--- a/solution.py
+++ b/solution.py
@@ -35,12 +35,16 @@
     n_tm,
     n_region,
     tiles,
+    flux_hbm,
+    penalty_hbm,
+    observed_hbm,
+    index_hbm,
+    footprint_ref,
+    out_ref,
     flux_ref,
     penalty_ref,
     observed_ref,
     index_ref,
-    footprint_ref,
-    out_ref,
     foot,
     foot_t,
     flux,
@@ -52,6 +56,12 @@
     all_terms,
     sums,
     parts,
+    base,
+    owned,
+    fields,
+    nearby,
+    whole_out,
+    whole_in,
     edges,
     edge_rows,
     edge_hours,
@@ -60,10 +70,12 @@
     pick,
     pick_t,
     foot_sem,
+    input_sem,
     pick_sem,
     send_sem,
     recv_sem,
     slot_recv,
+    side_sem,
     edge_send,
     edge_recv,
 ):
@@ -80,14 +92,27 @@
     partner = r + 1 - 2 * lax.rem(r, 2)
     near_first = [partner] + [2 * q + e for q in pairs[1:] for e in range(2)]
 
-    load = pltpu.make_async_copy(footprint_ref, foot, foot_sem)
-    load.start()
-
     barrier = pltpu.get_barrier_semaphore()
     for l, k in others:
         pl.semaphore_signal(
             barrier, inc=1, device_id={"tm": earlier[l], "region": region[k]}, device_id_type=MESH
         )
+    pl.semaphore_signal(barrier, inc=1, device_id={"tm": later[1], "region": r}, device_id_type=MESH)
+
+    inputs = [
+        pltpu.make_async_copy(src, dst, input_sem.at[k])
+        for k, (src, dst) in enumerate(
+            [
+                (flux_hbm, flux_ref),
+                (index_hbm, index_ref),
+                (observed_hbm, observed_ref),
+                (penalty_hbm, penalty_ref),
+            ]
+        )
+    ]
+    load = pltpu.make_async_copy(footprint_ref, foot, foot_sem)
+    for copy in inputs + [load]:
+        copy.start()
 
     def send(src, dst, sent, received, tm, reg):
         pltpu.make_async_remote_copy(
@@ -100,6 +125,9 @@
         ).start()
 
     index_pad[...] = jnp.zeros_like(index_pad)
+    all_terms[...] = jnp.zeros_like(all_terms)
+    for copy in inputs:
+        copy.wait()
     index_pad[0:4, 0:tiles] = index_ref[...]
     entries = index_pad[...]
     lag = entries[1:2, :]
@@ -108,39 +136,57 @@
     picks[r] = jnp.broadcast_to(mine, (8, 128))
     for h in range(HOURS):
         flux[0, h] = flux_ref[:, h, :]
-        low[0, h] = flux[0, h].astype(jnp.bfloat16)
-    all_terms[...] = jnp.zeros_like(all_terms)
-
-    pl.semaphore_wait(barrier, len(others))
+        low[h] = flux[0, h].astype(jnp.bfloat16)
+
+    pl.semaphore_wait(barrier, len(others) + 1)
+
+    def send_edges(i):
+        edges[i, 0] = flux[i, :, 0, :]
+        edges[i, 1] = flux[i, :, ROWS - 1, :]
+        for e, (src, dst, tm, reg) in enumerate(
+            [
+                (edges.at[i, 1], edge_rows.at[i, 0], w, region[1]),
+                (edges.at[i, 0], edge_rows.at[i, 1], w, region[n_region - 1]),
+                (flux.at[i, HOURS - 1], edge_hours.at[i, 0], later[1], r),
+                (flux.at[i, 0], edge_hours.at[i, 1], earlier[1], r),
+            ]
+        ):
+            send(src, dst, edge_send.at[i, e], edge_recv.at[i, e], tm, reg)
+
+    def make_base(i):
+        for e in range(2):
+            take(edge_rows.at[i, e], edge_recv.at[i, e])
+            take(edge_hours.at[i, e], edge_recv.at[i, 2 + e])
+        row_low = jnp.where(r > 0, edge_rows[i, 0], 0.0)
+        row_high = jnp.where(r < n_region - 1, edge_rows[i, 1], 0.0)
+        hour_low = jnp.where(w > 0, edge_hours[i, 0], 0.0)
+        hour_high = jnp.where(w < n_tm - 1, edge_hours[i, 1], 0.0)
+        cell = lax.broadcasted_iota(jnp.int32, (ROWS, CELLS), 1)
+        planes = [hour_low] + [flux[i, h] for h in range(HOURS)] + [hour_high]
+        for h in range(HOURS):
+            here = planes[h + 1]
+            neighbours = jnp.concatenate([here[1:], row_high[h : h + 1]], axis=0)
+            neighbours = neighbours + jnp.concatenate([row_low[h : h + 1], here[:-1]], axis=0)
+            neighbours = neighbours + planes[h + 2] + planes[h]
+            neighbours = neighbours + jnp.where(cell < CELLS - 1, pltpu.roll(here, CELLS - 1, 1), 0.0)
+            neighbours = neighbours + jnp.where(cell > 0, pltpu.roll(here, 1, 1), 0.0)
+            base[i, h] = here - 0.1 * (6.0 * here - neighbours)
+
+    def stepped(start, adjoint, cutoff):
+        value = start - 0.5 * adjoint
+        return value - jnp.clip(value, -cutoff, cutoff)
 
     for i in range(ITERS):
-        for l, k in others:
-            send(
-                low.at[i, region[k]],
-                window.at[i, l * n_region + r],
-                send_sem.at[i, 0],
-                recv_sem.at[i, 0],
-                later[l],
-                region[k],
-            )
-        window[i, r] = low[i, r]
         if i == 0:
+            for l, k in others:
+                send(
+                    low.at[region[k]], window.at[0, l * n_region + r],
+                    send_sem.at[0, 0], recv_sem.at[0, 0], later[l], region[k],
+                )
+            window[0, r] = low[r]
             for k in range(1, n_region):
                 send(picks.at[r], picks.at[r], pick_sem.at[0], pick_sem.at[1], w, region[k])
-        edges[i, 0] = flux[i, :, 0, :]
-        edges[i, 1] = flux[i, :, ROWS - 1, :]
-        send(
-            edges.at[i, 0], edge_rows.at[i, 1],
-            edge_send.at[i, 0], edge_recv.at[i, 0], w, region[n_region - 1],
-        )
-        send(
-            edges.at[i, 1], edge_rows.at[i, 0],
-            edge_send.at[i, 1], edge_recv.at[i, 1], w, region[1],
-        )
-        send(
-            flux.at[i, HOURS - 1], edge_hours.at[i, 0],
-            edge_send.at[i, 2], edge_recv.at[i, 2], later[1], r,
-        )
+            send_edges(0)
         if i == 0:
             load.wait()
             for t in range(tiles):
@@ -161,11 +207,11 @@
                 pick_t[:, d * SPREAD : (d + 2) * SPREAD] = chosen.astype(jnp.float32).astype(
                     jnp.bfloat16
                 )
-        take(window.at[i, 0 : len(others)], recv_sem.at[i, 0])
-        send(
-            flux.at[i, 0], edge_hours.at[i, 1],
-            edge_send.at[i, 3], edge_recv.at[i, 3], earlier[1], r,
-        )
+            make_base(0)
+            for h in range(HOURS):
+                owned[h, 0] = base[0, h].astype(jnp.bfloat16)
+                owned[h, 1] = (0.5 * penalty_ref[:, h, :]).astype(jnp.bfloat16)
+            take(window.at[0, 0 : len(others)], recv_sem.at[0, 0])
 
         table = window[i].reshape(table_rows, CELLS)
         blocks[i] = (
@@ -179,6 +225,17 @@
                 send_sem.at[i, 1], slot_recv.at[i, r], w, reg,
             )
         slots[i, r] = blocks[i, r]
+        if i == 0:
+            for l, k in others:
+                send(
+                    owned.at[region[k]], fields.at[l * n_region + r],
+                    side_sem.at[0, 0], side_sem.at[0, 1], later[l], region[k],
+                )
+            fields[r] = owned[r]
+        else:
+            for reg in reversed(near_first):
+                send(whole_out.at[reg], whole_in.at[r], side_sem.at[1, 0], side_sem.at[1, 1], w, reg)
+            whole_in[r] = whole_out[r]
 
         down = lax.broadcasted_iota(jnp.int32, (GROUP, OBS), 0)
         groups = [(first, min(first + GROUP, tiles)) for first in range(0, SLOTS, GROUP)]
@@ -232,6 +289,11 @@
                     send_sem.at[i, 2], recv_sem.at[i, 2], w, reg,
                 )
         all_terms[i, r, 0:SLOTS] = terms[i, r]
+        if i > 0:
+            take(whole_in.at[0 : n_region - 1], side_sem.at[1, 1])
+            for h in range(HOURS):
+                flux[i, h] = stepped(base[i - 1, h], whole_in[h], 0.5 * penalty_ref[:, h, :])
+            send_edges(i)
         take(all_terms.at[i, 0 : n_region - 1, 0:SLOTS], recv_sem.at[i, 2])
 
         received = all_terms[i].reshape(n_region * SPREAD, CELLS)
@@ -240,53 +302,56 @@
             .astype(jnp.bfloat16)
             .reshape(LAG * n_region, ROWS, CELLS)
         )
-        for l, k in others:
-            send(
-                sums.at[i, l * n_region + region[k]],
-                parts.at[i, l * n_region + r],
-                send_sem.at[i, 3],
-                recv_sem.at[i, 3],
-                earlier[l],
-                region[k],
-            )
-        parts[i, r] = sums[i, r]
-        for e in range(2):
-            take(edge_rows.at[i, e], edge_recv.at[i, e])
-            take(edge_hours.at[i, e], edge_recv.at[i, 2 + e])
-        take(parts.at[i, 0 : len(others)], recv_sem.at[i, 3])
-
-        row_low = jnp.where(r > 0, edge_rows[i, 0], 0.0)
-        row_high = jnp.where(r < n_region - 1, edge_rows[i, 1], 0.0)
-        hour_low = jnp.where(w > 0, edge_hours[i, 0], 0.0)
-        hour_high = jnp.where(w < n_tm - 1, edge_hours[i, 1], 0.0)
-        cell = lax.broadcasted_iota(jnp.int32, (ROWS, CELLS), 1)
-        planes = [hour_low] + [flux[i, h] for h in range(HOURS)] + [hour_high]
-        for h in range(HOURS):
-            here = planes[h + 1]
-            adjoint = parts[i, h].astype(jnp.float32)
-            for l in range(1, LAG):
-                adjoint = adjoint + parts[i, l * n_region + h].astype(jnp.float32)
-            neighbours = jnp.concatenate([here[1:], row_high[h : h + 1]], axis=0)
-            neighbours = neighbours + jnp.concatenate([row_low[h : h + 1], here[:-1]], axis=0)
-            neighbours = neighbours + planes[h + 2] + planes[h]
-            neighbours = neighbours + jnp.where(cell < CELLS - 1, pltpu.roll(here, CELLS - 1, 1), 0.0)
-            neighbours = neighbours + jnp.where(cell > 0, pltpu.roll(here, 1, 1), 0.0)
-            laplace = 6.0 * here - neighbours
-            stepped = here - 0.5 * (adjoint + 0.2 * laplace)
-            cutoff = 0.5 * penalty_ref[:, h, :]
-            new = stepped - jnp.clip(stepped, -cutoff, cutoff)
-            if i < ITERS - 1:
-                flux[i + 1, h] = new
-                low[i + 1, h] = new.astype(jnp.bfloat16)
-            else:
-                out_ref[:, h, :] = new
+        if i < ITERS - 1:
+            at, later_at, earlier_at = 0, {}, {}
+            for d in range(1, LAG):
+                size = (LAG - d) * n_region
+                later_at[d], earlier_at[d] = at, at + size
+                at += 2 * size
+                for src, start, tm in [(0, later_at[d], later[d]), (d * n_region, earlier_at[d], earlier[d])]:
+                    send(
+                        sums.at[i, src : src + size], nearby.at[start : start + size],
+                        side_sem.at[2, 0], side_sem.at[2, 1], tm, r,
+                    )
+            take(fields.at[0 : len(others)], side_sem.at[0, 1])
+            take(nearby, side_sem.at[2, 1])
+            for l in range(LAG):
+                rows_of = [(nearby, later_at[d] + (l - d) * n_region) for d in range(1, l + 1)]
+                rows_of += [(nearby, earlier_at[d] + l * n_region) for d in range(1, LAG - l)]
+                for g in range(n_region):
+                    adjoint = sums[i, l * n_region + g].astype(jnp.float32)
+                    for ref, start in rows_of:
+                        adjoint = adjoint + ref[start + g].astype(jnp.float32)
+                    if l == 0:
+                        whole_out[g] = adjoint
+                    field = fields[l * n_region + g].astype(jnp.float32)
+                    window[i + 1, l * n_region + g] = stepped(field[0], adjoint, field[1]).astype(
+                        jnp.bfloat16
+                    )
+        else:
+            for l, k in others:
+                send(
+                    sums.at[i, l * n_region + region[k]], parts.at[l * n_region + r],
+                    send_sem.at[i, 3], recv_sem.at[i, 3], earlier[l], region[k],
+                )
+            parts[r] = sums[i, r]
+            make_base(i)
+            take(parts.at[0 : len(others)], recv_sem.at[i, 3])
+            for h in range(HOURS):
+                adjoint = parts[h].astype(jnp.float32)
+                for l in range(1, LAG):
+                    adjoint = adjoint + parts[l * n_region + h].astype(jnp.float32)
+                out_ref[:, h, :] = stepped(base[i, h], adjoint, 0.5 * penalty_ref[:, h, :])
 
     take(picks.at[0 : n_region - 1], pick_sem.at[0])
+    take(window.at[0, 0 : len(others)], send_sem.at[0, 0])
+    take(fields.at[0 : len(others)], side_sem.at[0, 0])
+    take(whole_in.at[0 : n_region - 1], side_sem.at[1, 0])
+    take(nearby, side_sem.at[2, 0])
+    take(parts.at[0 : len(others)], send_sem.at[ITERS - 1, 3])
     for i in range(ITERS):
-        take(window.at[i, 0 : len(others)], send_sem.at[i, 0])
         take(slots.at[i, 0 : n_region - 1], send_sem.at[i, 1])
         take(terms.at[i, 0 : n_region - 1], send_sem.at[i, 2])
-        take(parts.at[i, 0 : len(others)], send_sem.at[i, 3])
         for e in range(2):
             take(edge_rows.at[i, e], edge_send.at[i, e])
             take(edge_hours.at[i, e], edge_send.at[i, 2 + e])
@@ -302,20 +367,30 @@
     return pl.pallas_call(
         functools.partial(kernel, n_tm, n_region, tiles),
         out_shape=jax.ShapeDtypeStruct(flux_init.shape, full),
-        in_specs=[in_vmem] * 4 + [pl.BlockSpec(memory_space=pl.ANY)],
+        in_specs=[pl.BlockSpec(memory_space=pltpu.HBM)] * 5,
         out_specs=in_vmem,
         scratch_shapes=[
+            pltpu.VMEM(flux_init.shape, full),
+            pltpu.VMEM(flux_init.shape, full),
+            pltpu.VMEM((NOB, OBS), full),
+            pltpu.VMEM((4, tiles), jnp.int32),
             pltpu.VMEM((tiles * OBS, HOURS * CELLS), half),
             pltpu.VMEM((HOURS * CELLS, tiles * OBS), half),
             pltpu.VMEM((ITERS, HOURS, ROWS, CELLS), full),
-            pltpu.VMEM((ITERS, HOURS, ROWS, CELLS), half),
+            pltpu.VMEM((HOURS, ROWS, CELLS), half),
             pltpu.VMEM((ITERS, table, ROWS, CELLS), half),
             pltpu.VMEM((ITERS, n_region, SLOTS, CELLS), half),
             pltpu.VMEM((ITERS, n_region, SLOTS, CELLS), half),
             pltpu.VMEM((ITERS, n_region, SLOTS, CELLS), half),
             pltpu.VMEM((ITERS, n_region, SPREAD, CELLS), half),
             pltpu.VMEM((ITERS, table, ROWS, CELLS), half),
-            pltpu.VMEM((ITERS, table, ROWS, CELLS), half),
+            pltpu.VMEM((table, ROWS, CELLS), half),
+            pltpu.VMEM((ITERS, HOURS, ROWS, CELLS), full),
+            pltpu.VMEM((HOURS, 2, ROWS, CELLS), half),
+            pltpu.VMEM((table, 2, ROWS, CELLS), half),
+            pltpu.VMEM((LAG * (LAG - 1) * n_region, ROWS, CELLS), half),
+            pltpu.VMEM((n_region, ROWS, CELLS), full),
+            pltpu.VMEM((n_region, ROWS, CELLS), full),
             pltpu.VMEM((ITERS, 2, HOURS, CELLS), full),
             pltpu.VMEM((ITERS, 2, HOURS, CELLS), full),
             pltpu.VMEM((ITERS, 2, ROWS, CELLS), full),
@@ -324,10 +399,12 @@
             pltpu.VMEM((n_region * SLOTS, table * ROWS), half),
             pltpu.VMEM((table * ROWS, n_region * SPREAD), half),
             dma,
+            dma((4,)),
             dma((2,)),
             dma((ITERS, 4)),
             dma((ITERS, 4)),
             dma((ITERS, n_region)),
+            dma((3, 2)),
             dma((ITERS, 4)),
             dma((ITERS, 4)),
         ],

time: 60 us -> 52.1 us (0.87)
  Pallas kernels: 58.3 us -> 50.5 us
    pallas_call x1, Pallas kernels: 58.3 us -> 50.5 us  [local(): pl.pallas_call(functools.partial(kernel, n_tm, n_region, tiles), out_shap...]
where the time goes in v3:
time: 52.1 us; the launch traced here: 52 us
  Pallas kernels  50.5 us (97%)
  local copies, waits for them, and re-layouts  1.47 us (3%)
    pallas_call x1, Pallas kernels, local(): pl.pallas_call(functools.partial(kernel, n_tm, n_region, tiles), out_shap...  50.5 us
    unnamed x1, local copies, waits for them, and re-layouts  1.47 us

profile of v3, /device:TPU:1, one launch (start us, length us, event | category | flops | bytes accessed | tf_op | source)
XLA Modules:
  0.0 52.0 jit_solution(18014808491991070693)
XLA Ops:
  0.0 50.5 %shard_map.55 = f32[16,8,128]{2,1,0:T(8,128)} custom-call(f32[16,8,128]{2,1,0:T(8,128)} %flux_hbm.1, f32[16,8,128]{2,1,0:T(8,128)} %penalty_hbm.1, f32[8,128]{1,0:T(8,128)} %bitcast.4, s32[4,40]{1,0:T(4,128)} %bitcast.5, bf16[5120,1024]{1,0:T(8,128)(2,1)} %bitcast.3), custom_call_target="tpu_custom_call" | custom-call | flops 41943040 | bytes 10485760 | tf_op jit(solution)/shard_map/pallas_call | solution.py:367
  50.5 1.5 %copy.7 = f32[16,8,128]{2,1,0:T(8,128)} copy(f32[16,8,128]{2,1,0:T(8,128)} %shard_map.55) | data formatting | bytes 131072

commit v4 on v3

--- a/solution.py
+++ b/solution.py
@@ -189,8 +189,16 @@
             send_edges(0)
         if i == 0:
             load.wait()
-            for t in range(tiles):
+            for t in range(24):
                 foot_t[:, t * OBS : (t + 1) * OBS] = jnp.transpose(foot[t * OBS : (t + 1) * OBS, :])
+            for h in range(HOURS):
+                owned[h, 1] = (0.5 * penalty_ref[:, h, :]).astype(jnp.bfloat16)
+            for l, k in others:
+                send(
+                    owned.at[region[k], 1], fields.at[l * n_region + r, 1],
+                    side_sem.at[0, 0], side_sem.at[0, 1], later[l], region[k],
+                )
+            fields[r, 1] = owned[r, 1]
             take(picks.at[0 : n_region - 1], pick_sem.at[1])
             rows = picks[:, 0, :]
             columns = jnp.transpose(jnp.concatenate([rows] * 16, axis=0))
@@ -210,28 +218,29 @@
             make_base(0)
             for h in range(HOURS):
                 owned[h, 0] = base[0, h].astype(jnp.bfloat16)
-                owned[h, 1] = (0.5 * penalty_ref[:, h, :]).astype(jnp.bfloat16)
             take(window.at[0, 0 : len(others)], recv_sem.at[0, 0])
 
         table = window[i].reshape(table_rows, CELLS)
-        blocks[i] = (
-            dot(pick[...], table, ((1,), (0,)))
-            .astype(jnp.bfloat16)
-            .reshape(n_region, SLOTS, CELLS)
-        )
-        for reg in reversed(near_first):
-            send(
-                blocks.at[i, reg], slots.at[i, r],
-                send_sem.at[i, 1], slot_recv.at[i, r], w, reg,
-            )
+        for q in reversed(pairs):
+            rows_of = pl.ds(pl.multiple_of(q * 2 * SLOTS, 2 * SLOTS), 2 * SLOTS)
+            both = dot(pick[rows_of, :], table, ((1,), (0,))).astype(jnp.bfloat16)
+            blocks[i, 2 * q] = both[:SLOTS]
+            blocks[i, 2 * q + 1] = both[SLOTS:]
+            for reg in [2 * q + 1, 2 * q] if q is not own else [partner]:
+                send(
+                    blocks.at[i, reg], slots.at[i, r],
+                    send_sem.at[i, 1], slot_recv.at[i, r], w, reg,
+                )
         slots[i, r] = blocks[i, r]
         if i == 0:
             for l, k in others:
                 send(
-                    owned.at[region[k]], fields.at[l * n_region + r],
+                    owned.at[region[k], 0], fields.at[l * n_region + r, 0],
                     side_sem.at[0, 0], side_sem.at[0, 1], later[l], region[k],
                 )
-            fields[r] = owned[r]
+            fields[r, 0] = owned[r, 0]
+            for t in range(24, tiles):
+                foot_t[:, t * OBS : (t + 1) * OBS] = jnp.transpose(foot[t * OBS : (t + 1) * OBS, :])
         else:
             for reg in reversed(near_first):
                 send(whole_out.at[reg], whole_in.at[r], side_sem.at[1, 0], side_sem.at[1, 1], w, reg)
@@ -297,22 +306,39 @@
         take(all_terms.at[i, 0 : n_region - 1, 0:SLOTS], recv_sem.at[i, 2])
 
         received = all_terms[i].reshape(n_region * SPREAD, CELLS)
-        sums[i] = (
-            dot(pick_t[...], received, ((1,), (0,)))
-            .astype(jnp.bfloat16)
-            .reshape(LAG * n_region, ROWS, CELLS)
-        )
+        lag_rows = n_region * ROWS
+        at, later_at, earlier_at = 0, {}, {}
+        for d in range(1, LAG):
+            size = (LAG - d) * n_region
+            later_at[d], earlier_at[d] = at, at + size
+            at += 2 * size
+        ready = set()
+        waiting = [(d, side) for d in reversed(range(1, LAG)) for side in (0, 1)]
+        for l in [3, 0, 1, 2] if i < ITERS - 1 else [3, 2, 1, 0]:
+            part = dot(pick_t[l * lag_rows : (l + 1) * lag_rows, :], received, ((1,), (0,)))
+            sums[i, l * n_region : (l + 1) * n_region] = part.astype(jnp.bfloat16).reshape(
+                n_region, ROWS, CELLS
+            )
+            ready.add(l)
+            for d, side in list(waiting) if i < ITERS - 1 else []:
+                first = d * side
+                if not ready.issuperset(range(first, first + LAG - d)):
+                    continue
+                waiting.remove((d, side))
+                size = (LAG - d) * n_region
+                start = earlier_at[d] if side else later_at[d]
+                send(
+                    sums.at[i, first * n_region : first * n_region + size],
+                    nearby.at[start : start + size],
+                    side_sem.at[2, 0], side_sem.at[2, 1], earlier[d] if side else later[d], r,
+                )
+            if i == ITERS - 1:
+                for k in reversed(range(1 if l == 0 else 0, n_region)):
+                    send(
+                        sums.at[i, l * n_region + region[k]], parts.at[l * n_region + r],
+                        send_sem.at[i, 3], recv_sem.at[i, 3], earlier[l], region[k],
+                    )
         if i < ITERS - 1:
-            at, later_at, earlier_at = 0, {}, {}
-            for d in range(1, LAG):
-                size = (LAG - d) * n_region
-                later_at[d], earlier_at[d] = at, at + size
-                at += 2 * size
-                for src, start, tm in [(0, later_at[d], later[d]), (d * n_region, earlier_at[d], earlier[d])]:
-                    send(
-                        sums.at[i, src : src + size], nearby.at[start : start + size],
-                        side_sem.at[2, 0], side_sem.at[2, 1], tm, r,
-                    )
             take(fields.at[0 : len(others)], side_sem.at[0, 1])
             take(nearby, side_sem.at[2, 1])
             for l in range(LAG):
@@ -329,11 +355,6 @@
                         jnp.bfloat16
                     )
         else:
-            for l, k in others:
-                send(
-                    sums.at[i, l * n_region + region[k]], parts.at[l * n_region + r],
-                    send_sem.at[i, 3], recv_sem.at[i, 3], earlier[l], region[k],
-                )
             parts[r] = sums[i, r]
             make_base(i)
             take(parts.at[0 : len(others)], recv_sem.at[i, 3])

time: 52.1 us -> 50.2 us (0.964)
  Pallas kernels: 50.5 us -> 48.6 us
    pallas_call x1, Pallas kernels: 50.5 us -> 48.6 us  [local(): pl.pallas_call(functools.partial(kernel, n_tm, n_region, tiles), out_shap...]
where the time goes in v4:
time: 50.2 us; the launch traced here: 50.1 us
  Pallas kernels  48.6 us (97%)
  local copies, waits for them, and re-layouts  1.47 us (3%)
    pallas_call x1, Pallas kernels, local(): pl.pallas_call(functools.partial(kernel, n_tm, n_region, tiles), out_shap...  48.6 us
    unnamed x1, local copies, waits for them, and re-layouts  1.47 us

profile of v4, /device:TPU:1, one launch (start us, length us, event | category | flops | bytes accessed | tf_op | source)
XLA Modules:
  0.0 50.1 jit_solution(3953261419451843842)
XLA Ops:
  0.0 48.6 %shard_map.55 = f32[16,8,128]{2,1,0:T(8,128)} custom-call(f32[16,8,128]{2,1,0:T(8,128)} %flux_hbm.1, f32[16,8,128]{2,1,0:T(8,128)} %penalty_hbm.1, f32[8,128]{1,0:T(8,128)} %bitcast.4, s32[4,40]{1,0:T(4,128)} %bitcast.5, bf16[5120,1024]{1,0:T(8,128)(2,1)} %bitcast.3), custom_call_target="tpu_custom_call" | custom-call | flops 41943040 | bytes 10485760 | tf_op jit(solution)/shard_map/pallas_call | solution.py:388
  48.6 1.5 %copy.7 = f32[16,8,128]{2,1,0:T(8,128)} copy(f32[16,8,128]{2,1,0:T(8,128)} %shard_map.55) | data formatting | bytes 131072

commit v5 on v4

--- a/solution.py
+++ b/solution.py
@@ -178,11 +178,12 @@
 
     for i in range(ITERS):
         if i == 0:
-            for l, k in others:
-                send(
-                    low.at[region[k]], window.at[0, l * n_region + r],
-                    send_sem.at[0, 0], recv_sem.at[0, 0], later[l], region[k],
-                )
+            for l in reversed(range(LAG)):
+                for reg in near_first[::-1] + ([r] if l else []):
+                    send(
+                        low.at[reg], window.at[0, l * n_region + r],
+                        send_sem.at[0, 0], recv_sem.at[0, 0], later[l], reg,
+                    )
             window[0, r] = low[r]
             for k in range(1, n_region):
                 send(picks.at[r], picks.at[r], pick_sem.at[0], pick_sem.at[1], w, region[k])
@@ -333,10 +334,10 @@
                     side_sem.at[2, 0], side_sem.at[2, 1], earlier[d] if side else later[d], r,
                 )
             if i == ITERS - 1:
-                for k in reversed(range(1 if l == 0 else 0, n_region)):
+                for reg in near_first[::-1] + ([r] if l else []):
                     send(
-                        sums.at[i, l * n_region + region[k]], parts.at[l * n_region + r],
-                        send_sem.at[i, 3], recv_sem.at[i, 3], earlier[l], region[k],
+                        sums.at[i, l * n_region + reg], parts.at[l * n_region + r],
+                        send_sem.at[i, 3], recv_sem.at[i, 3], earlier[l], reg,
                     )
         if i < ITERS - 1:
             take(fields.at[0 : len(others)], side_sem.at[0, 1])

time: 50.2 us -> 50 us (level)
  no operation moved by 1% of the time
where the time goes in v5:
time: 50 us; the launch traced here: 49.9 us
  Pallas kernels  48.4 us (97%)
  local copies, waits for them, and re-layouts  1.47 us (3%)
    pallas_call x1, Pallas kernels, local(): pl.pallas_call(functools.partial(kernel, n_tm, n_region, tiles), out_shap...  48.4 us
    unnamed x1, local copies, waits for them, and re-layouts  1.47 us

profile of v5, /device:TPU:1, one launch (start us, length us, event | category | flops | bytes accessed | tf_op | source)
XLA Modules:
  0.0 49.9 jit_solution(2625159658160393924)
XLA Ops:
  0.0 48.4 %shard_map.55 = f32[16,8,128]{2,1,0:T(8,128)} custom-call(f32[16,8,128]{2,1,0:T(8,128)} %flux_hbm.1, f32[16,8,128]{2,1,0:T(8,128)} %penalty_hbm.1, f32[8,128]{1,0:T(8,128)} %bitcast.4, s32[4,40]{1,0:T(4,128)} %bitcast.5, bf16[5120,1024]{1,0:T(8,128)(2,1)} %bitcast.3), custom_call_target="tpu_custom_call" | custom-call | flops 41943040 | bytes 10485760 | tf_op jit(solution)/shard_map/pallas_call | solution.py:389
  48.4 1.5 %copy.7 = f32[16,8,128]{2,1,0:T(8,128)} copy(f32[16,8,128]{2,1,0:T(8,128)} %shard_map.55) | data formatting | bytes 131072

commit v6 on v5

--- a/solution.py
+++ b/solution.py
@@ -18,17 +18,14 @@
 NOB = 8
 GROUP = 16
 MESH = pl.DeviceIdType.MESH
-HIGHEST = lax.Precision.HIGHEST
 
 
 def take(ref, sem):
     pltpu.make_async_copy(ref, ref, sem).wait()
 
 
-def dot(a, b, dims, precision=None):
-    return lax.dot_general(
-        a, b, (dims, ((), ())), precision=precision, preferred_element_type=jnp.float32
-    )
+def dot(a, b, dims):
+    return lax.dot_general(a, b, (dims, ((), ())), preferred_element_type=jnp.float32)
 
 
 def kernel(
@@ -66,6 +63,7 @@
     edge_rows,
     edge_hours,
     index_pad,
+    block_of,
     picks,
     pick,
     pick_t,
@@ -216,6 +214,7 @@
                 pick_t[:, d * SPREAD : (d + 2) * SPREAD] = chosen.astype(jnp.float32).astype(
                     jnp.bfloat16
                 )
+            block_of[...] = jnp.broadcast_to(jnp.transpose(index_pad[...])[0:SLOTS, 0:1], (SLOTS, OBS))
             make_base(0)
             for h in range(HOURS):
                 owned[h, 0] = base[0, h].astype(jnp.bfloat16)
@@ -264,15 +263,16 @@
                     total = jnp.where(down == t + 1 - first, both[:, OBS:], total)
                 products[g] = products[g] + total
         products = jnp.concatenate(products, axis=0)
-        row_block = index_pad[0:1, 0:SLOTS]
-        selector = (lax.broadcasted_iota(jnp.int32, (NOB, SLOTS), 0) == row_block).astype(jnp.float32)
-        predicted = dot(selector, products, ((1,), (0,)), HIGHEST)
-        residual = (predicted - observed_ref[...]).astype(jnp.bfloat16).astype(jnp.float32)
+        residual = []
+        for b in range(NOB):
+            predicted = jnp.sum(jnp.where(block_of[...] == b, products, 0.0), axis=0, keepdims=True)
+            residual.append(
+                (predicted - observed_ref[b : b + 1, :]).astype(jnp.bfloat16).astype(jnp.float32)
+            )
 
         spread = jnp.zeros((SLOTS, OBS), jnp.float32)
-        block_of = jnp.transpose(index_pad[...])[0:SLOTS, 0:1]
         for b in range(NOB):
-            spread = jnp.where(block_of == b, residual[b : b + 1, :], spread)
+            spread = jnp.where(block_of[...] == b, residual[b], spread)
         lefts = []
         for first in range(0, SLOTS, GROUP):
             part = spread[first : first + GROUP, :]
@@ -363,7 +363,7 @@
                 adjoint = parts[h].astype(jnp.float32)
                 for l in range(1, LAG):
                     adjoint = adjoint + parts[l * n_region + h].astype(jnp.float32)
-                out_ref[:, h, :] = stepped(base[i, h], adjoint, 0.5 * penalty_ref[:, h, :])
+                out_ref[:, h, :] = base[i, h] - 0.5 * adjoint
 
     take(picks.at[0 : n_region - 1], pick_sem.at[0])
     take(window.at[0, 0 : len(others)], send_sem.at[0, 0])
@@ -386,7 +386,7 @@
     table = LAG * n_region
     half, full = jnp.bfloat16, jnp.float32
     dma = pltpu.SemaphoreType.DMA
-    return pl.pallas_call(
+    last = pl.pallas_call(
         functools.partial(kernel, n_tm, n_region, tiles),
         out_shape=jax.ShapeDtypeStruct(flux_init.shape, full),
         in_specs=[pl.BlockSpec(memory_space=pltpu.HBM)] * 5,
@@ -417,6 +417,7 @@
             pltpu.VMEM((ITERS, 2, HOURS, CELLS), full),
             pltpu.VMEM((ITERS, 2, ROWS, CELLS), full),
             pltpu.VMEM((128, 128), jnp.int32),
+            pltpu.VMEM((SLOTS, OBS), jnp.int32),
             pltpu.VMEM((n_region, 8, 128), jnp.int32),
             pltpu.VMEM((n_region * SLOTS, table * ROWS), half),
             pltpu.VMEM((table * ROWS, n_region * SPREAD), half),
@@ -443,6 +444,8 @@
         tile_index.T,
         footprint.reshape(tiles * OBS, HOURS * CELLS),
     )
+    cutoff = 0.5 * penalty
+    return last - jnp.clip(last, -cutoff, cutoff)
 
 
 def solution(mesh):

time: 50 us -> 49.7 us (level)
  other arithmetic: 0 us -> 1.48 us
  local copies, waits for them, and re-layouts: 1.47 us -> 0.01 us
    sub x0 -> x1, other arithmetic: none -> 1.48 us  [local(): return last - jnp.clip(last, -cutoff, cutoff)]
    unnamed x1 -> x2, local copies, waits for them, and re-layouts: 1.47 us -> 0.01 us
where the time goes in v6:
time: 49.7 us; the launch traced here: 49.6 us
  Pallas kernels  48.1 us (97%)
  other arithmetic  1.48 us (3%)
    pallas_call x1, Pallas kernels, local(): pl.pallas_call(functools.partial(kernel, n_tm, n_region, tiles), out_shap...  48.1 us
    sub x1, other arithmetic, local(): return last - jnp.clip(last, -cutoff, cutoff)  1.48 us

profile of v6, /device:TPU:1, one launch (start us, length us, event | category | flops | bytes accessed | tf_op | source)
XLA Modules:
  0.0 49.6 jit_solution(7373982696089744681)
XLA Ops:
  0.0 0.0 copy-start
  0.0 48.1 %shard_map.55 = f32[16,8,128]{2,1,0:T(8,128)} custom-call(f32[16,8,128]{2,1,0:T(8,128)} %flux_hbm.1, f32[16,8,128]{2,1,0:T(8,128)} %penalty_hbm.1, f32[8,128]{1,0:T(8,128)} %bitcast.4, s32[4,40]{1,0:T(4,128)} %bitcast.5, bf16[5120,1024]{1,0:T(8,128)(2,1)} %bitcast.3), custom_call_target="tpu_custom_call" | custom-call | flops 41943040 | bytes 10485760 | tf_op jit(solution)/shard_map/pallas_call | solution.py:389
  48.1 0.0 copy-done
  48.1 1.5 %minimum_subtract_fusion = f32[16,8,128]{2,1,0:T(8,128)} fusion(f32[16,8,128]{2,1,0:T(8,128)} %shard_map.55, f32[16,8,128]{2,1,0:T(8,128)S(1)} %copy-done), kind=kLoop, calls=%fused_computation | loop fusion | flops 81920 | bytes 196608 | tf_op jit(solution)/shard_map/sub | solution.py:448
Async XLA Ops:
  0.0 48.1 %copy-start = (f32[16,8,128]{2,1,0:T(8,128)S(1)}, f32[16,8,128]{2,1,0:T(8,128)}, u32[]{:S(2)}) copy-start(f32[16,8,128]{2,1,0:T(8,128)} %penalty_hbm.1) | copy-start | bytes 196612

commit v7 on v6

--- a/solution.py
+++ b/solution.py
@@ -122,16 +122,7 @@
             device_id_type=MESH,
         ).start()
 
-    index_pad[...] = jnp.zeros_like(index_pad)
-    all_terms[...] = jnp.zeros_like(all_terms)
-    for copy in inputs:
-        copy.wait()
-    index_pad[0:4, 0:tiles] = index_ref[...]
-    entries = index_pad[...]
-    lag = entries[1:2, :]
-    usable = (entries[3:4, :] == 1) & (lag <= w)
-    mine = jnp.where(usable, lag * (n_region * ROWS) + entries[2:3, :], -1)
-    picks[r] = jnp.broadcast_to(mine, (8, 128))
+    inputs[0].wait()
     for h in range(HOURS):
         flux[0, h] = flux_ref[:, h, :]
         low[h] = flux[0, h].astype(jnp.bfloat16)
@@ -183,9 +174,20 @@
                         send_sem.at[0, 0], recv_sem.at[0, 0], later[l], reg,
                     )
             window[0, r] = low[r]
+            index_pad[...] = jnp.zeros_like(index_pad)
+            inputs[1].wait()
+            index_pad[0:4, 0:tiles] = index_ref[...]
+            entries = index_pad[...]
+            lag = entries[1:2, :]
+            usable = (entries[3:4, :] == 1) & (lag <= w)
+            mine = jnp.where(usable, lag * (n_region * ROWS) + entries[2:3, :], -1)
+            picks[r] = jnp.broadcast_to(mine, (8, 128))
             for k in range(1, n_region):
                 send(picks.at[r], picks.at[r], pick_sem.at[0], pick_sem.at[1], w, region[k])
             send_edges(0)
+            all_terms[...] = jnp.zeros_like(all_terms)
+            for copy in inputs[2:]:
+                copy.wait()
         if i == 0:
             load.wait()
             for t in range(24):

time: 49.7 us -> 49.7 us (level)
  no operation moved by 1% of the time
where the time goes in v7:
time: 49.7 us; the launch traced here: 49.6 us
  Pallas kernels  48.1 us (97%)
  other arithmetic  1.48 us (3%)
    pallas_call x1, Pallas kernels, local(): pl.pallas_call(functools.partial(kernel, n_tm, n_region, tiles), out_shap...  48.1 us
    sub x1, other arithmetic, local(): return last - jnp.clip(last, -cutoff, cutoff)  1.48 us

profile of v7, /device:TPU:1, one launch (start us, length us, event | category | flops | bytes accessed | tf_op | source)
XLA Modules:
  0.0 49.6 jit_solution(7013159975315880863)
XLA Ops:
  0.0 0.0 copy-start
  0.0 48.1 %shard_map.55 = f32[16,8,128]{2,1,0:T(8,128)} custom-call(f32[16,8,128]{2,1,0:T(8,128)} %flux_hbm.1, f32[16,8,128]{2,1,0:T(8,128)} %penalty_hbm.1, f32[8,128]{1,0:T(8,128)} %bitcast.4, s32[4,40]{1,0:T(4,128)} %bitcast.5, bf16[5120,1024]{1,0:T(8,128)(2,1)} %bitcast.3), custom_call_target="tpu_custom_call" | custom-call | flops 41943040 | bytes 10485760 | tf_op jit(solution)/shard_map/pallas_call | solution.py:391
  48.1 0.0 copy-done
  48.1 1.5 %minimum_subtract_fusion = f32[16,8,128]{2,1,0:T(8,128)} fusion(f32[16,8,128]{2,1,0:T(8,128)} %shard_map.55, f32[16,8,128]{2,1,0:T(8,128)S(1)} %copy-done), kind=kLoop, calls=%fused_computation | loop fusion | flops 81920 | bytes 196608 | tf_op jit(solution)/shard_map/sub | solution.py:450
Async XLA Ops:
  0.0 48.1 %copy-start = (f32[16,8,128]{2,1,0:T(8,128)S(1)}, f32[16,8,128]{2,1,0:T(8,128)}, u32[]{:S(2)}) copy-start(f32[16,8,128]{2,1,0:T(8,128)} %penalty_hbm.1) | copy-start | bytes 196612
